TPU v7x, 128 devices: a whole 4x4x4 slice. The times are simulated.
128 devices in a mesh: rep: 2 (over z_hi), section: 8 (over x, core), tp: 8 (over y, z_lo).
Axes of the slice: x: 4, y: 4, z: 4 (z_hi: 2, z_lo: 2; z = z_hi * 2 + z_lo), core: 2. Of those that a mesh axis runs over, the one named last changes fastest.
Arguments:
- section_map: int32 [2, 8], replicated, may hold values from 0 to 7, as said below
- checkpoint: bfloat16 [2, 8, 2, 64, 4096], P('rep', 'section'), may hold values from -6 to 6
- top_grad: bfloat16 [2, 2, 64, 4096], P('rep'), may hold values from -6 to 6
- value_weight: bfloat16 [2, 16, 4096, 4096], P('rep', 'section', None, 'tp'), may hold values from -0.09375 to 0.09375
- out_weight: bfloat16 [2, 16, 4096, 4096], P('rep', 'section', None, 'tp'), may hold values from -0.09375 to 0.09375
Outputs:
- value_grad: bfloat16 [8, 4096, 4096], P(None, ('rep', 'section'), 'tp')
- out_grad: bfloat16 [8, 4096, 4096], P(None, ('rep', 'section'), 'tp')
Inputs may be any that keep to these rules, and one draw needn't show every extreme that they name: `section_map`: row r lists the section of each layer for replica r; entries never fall along a row; a section holds at most 2 layers and may hold none.
All inputs are finite; a program needn't handle non-finite values.
Results may differ from a plain program's by a relative error of at most 0.035.
Values may be sent and summed in bfloat16 or wider, within the bound.
No kernel may reach another device: no remote copies, remote signals or barrier semaphores. Data moves between devices by JAX's collectives and lax.ppermute only.
A program may use at most 192 MiB of HBM per device.

v0:
```python
import functools

import jax
import jax.numpy as jnp
from jax import lax
from jax.experimental import pallas as pl
from jax.experimental.pallas import tpu as pltpu
from jax.sharding import PartitionSpec as P

BF16 = jnp.bfloat16
F32 = jnp.float32
VMEM_BYTES = 64 * 1024 * 1024
NT = (((1,), (1,)), ((), ()))
TN = (((0,), (0,)), ((), ()))
ANY = pl.BlockSpec(memory_space=pl.ANY)
HBM = pl.BlockSpec(memory_space=pltpu.HBM)
SMEM = pl.BlockSpec(memory_space=pltpu.SMEM)
VMEM = pl.BlockSpec(memory_space=pltpu.VMEM)


REP, CHIP, CORE, SIDE, TP = range(5)


def held_at(ids, section_map, layer):
    section = section_map[ids[REP], layer]
    slot = jnp.int32(0)
    if layer > 0:
        slot = (section_map[ids[REP], layer - 1] == section).astype(jnp.int32)
    chips = 4
    return lax.rem(section, 2), slot, lax.rem(section // 2 - ids[CHIP] + chips, chips)


def silu_slope(preact):
    sigma = jax.nn.sigmoid(preact)
    return sigma * (1.0 + preact * (1.0 - sigma))


def run(kernel, operands, specs, outs, out_specs, scratch, bytes_moved, flops=0):
    return pl.pallas_call(
        kernel,
        out_shape=outs,
        in_specs=specs,
        out_specs=out_specs,
        scratch_shapes=scratch,
        compiler_params=pltpu.CompilerParams(vmem_limit_bytes=VMEM_BYTES),
        cost_estimate=pl.CostEstimate(flops=flops, bytes_accessed=bytes_moved, transcendentals=0),
    )(*operands)


def rows_place(ref, cut, core):
    if len(ref.shape) == 3 and ref.shape[-1] == cut:
        return lambda i: ref.at[i]
    columns = lambda i: pl.ds(pl.multiple_of(i * cut, cut), cut)
    if len(ref.shape) == 2:
        return lambda i: ref.at[:, columns(i)]
    return lambda i: ref.at[core, :, columns(i)]


class Copies:
    def __init__(self, sems):
        self.sems, self.all = sems, []

    def start(self, source, target, condition=None):
        copy = pltpu.make_async_copy(source, target, self.sems.at[len(self.all)])
        if condition is None:
            copy.start()
        else:
            pl.when(condition)(copy.start)
        self.all.append(copy)
        return copy

    def either(self, condition, first, second, target):
        sem = self.sems.at[len(self.all)]
        pl.when(condition)(lambda: pltpu.make_async_copy(first, target, sem).start())
        pl.when(jnp.logical_not(condition))(lambda: pltpu.make_async_copy(second, target, sem).start())
        self.all.append(pltpu.make_async_copy(first, target, sem))
        return self.all[-1]

    def wait(self):
        for copy in self.all:
            copy.wait()


def halves(ref):
    step = ref.shape[0] // 2
    return [pl.ds(i * step, step) for i in range(2)]


def product_in(rows, weight, waits):
    cuts, cut = rows.shape[0], rows.shape[-1]
    total = None
    for i in range(cuts):
        if i % (cuts // len(waits)) == 0:
            waits[i // (cuts // len(waits))].wait()
        part = jnp.dot(rows[i], weight[i * cut : (i + 1) * cut, :], preferred_element_type=F32)
        total = part if total is None else total + part
    return total


def product_out(rows, weight, waits, stage, part_ref, out):
    cuts, cut = stage.shape[0], stage.shape[-1]
    group = cuts // len(waits)
    for i in range(cuts):
        if i % group == 0:
            waits[i // group].wait()
        part = lax.dot_general(rows, weight[i * cut : (i + 1) * cut, :], NT, preferred_element_type=F32)
        stage[i] = part.astype(BF16)
        if i % group == group - 1:
            cuts_done = pl.ds(i - group + 1, group)
            out.start(stage.at[cuts_done], part_ref.at[cuts_done])


def recompute(chips, with_parts, slot, deps, ids, x_ref, v_ref, *refs):
    o_ref, refs = (refs[0], refs[1:]) if with_parts else (None, refs)
    refs = refs[deps:]
    part_ref, refs = (refs[0], refs[1:]) if with_parts else (None, refs)
    outs, (xbuf, vbuf, act_rows, slope_rows, in_sems, out_sems) = refs[:6], refs[6:12]
    cuts, cut = xbuf.shape[0], xbuf.shape[-1]
    core, side = ids[CORE], ids[SIDE]
    arriving, leaving = Copies(in_sems), Copies(out_sems)
    x = [arriving.start(rows_place(x_ref, cut, core)(i), xbuf.at[i]) for i in range(cuts)]
    v = [arriving.start(v_ref.at[slot, rows], vbuf.at[rows]) for rows in halves(vbuf)]
    if with_parts:
        obuf, stage = refs[12:]
        o = [arriving.start(o_ref.at[slot, rows], obuf.at[rows]) for rows in halves(obuf)]
    for copy in x:
        copy.wait()
    pre = product_in(xbuf, vbuf, v)
    act = jax.nn.silu(pre).astype(BF16)
    if with_parts:
        product_out(act, obuf, o, stage, part_ref, leaving)
    act_rows[...] = act
    slope_rows[...] = silu_slope(pre)
    half = outs[0].shape[0]
    quarter = cut // 4
    for k, which in enumerate((core, 1 - core)):
        rows = pl.ds(pl.multiple_of(which * half, half), half)
        act_out, slope_out, x_out = outs[k], outs[2 + k], outs[4 + k]
        act_out[...] = act_rows[rows, :]
        slope_out[...] = slope_rows[rows, :]
        for to in range(chips):
            for j in range(4):
                columns = pl.ds(pl.multiple_of((j % 2) * 2 * quarter + side * quarter, quarter), quarter)
                x_out[to, :, j * quarter : (j + 1) * quarter] = xbuf[(j // 2) * chips + to, rows, columns]
    leaving.wait()


def step(chips, layer, deps, ids, section_map, g_ref, *refs):
    with_parts = layer > 0
    slopes, refs = refs[:4], refs[4:]
    o_refs, refs = refs[:2], refs[2:]
    v_refs, refs = (refs[:2], refs[2:]) if with_parts else (None, refs)
    refs = refs[deps:]
    part_ref, refs = (refs[0], refs[1:]) if with_parts else (None, refs)
    outs, (gbuf, sbuf, obuf, pay, in_sems, out_sems) = refs[:chips], refs[chips : chips + 6]
    cut, width = gbuf.shape[-1], sbuf.shape[-1]
    span = (pay.shape[-1] - width) // 4
    chip, core, side = ids[CHIP], ids[CORE], ids[SIDE]
    section_core, slot, _ = held_at(ids, section_map, layer)
    own = section_core == core
    arriving, leaving = Copies(in_sems), Copies(out_sems)
    if g_ref.shape == gbuf.shape:
        g = [arriving.start(g_ref, gbuf)]
    else:
        g = [arriving.start(rows_place(g_ref, cut, core)(i), gbuf.at[i]) for i in range(gbuf.shape[0])]
    o = [arriving.either(own, o_refs[0].at[slot, r], o_refs[1].at[slot, r], obuf.at[r]) for r in halves(obuf)]
    which = jnp.where(own, 0, 2) + slot
    for j in range(4):
        pl.when(which == j)(pltpu.make_async_copy(slopes[j], sbuf, in_sems.at[-1 + in_sems.shape[0]]).start)
    slope = pltpu.make_async_copy(slopes[0], sbuf, in_sems.at[-1 + in_sems.shape[0]])
    if with_parts:
        vbuf, stage = refs[chips + 6 :]
        v = [arriving.either(own, v_refs[0].at[slot, r], v_refs[1].at[slot, r], vbuf.at[r]) for r in halves(vbuf)]
    for copy in g:
        copy.wait()
    for far in range(chips):
        to = lax.rem(chip + far, chips)
        for j in range(4):
            start = (j % 2) * (cut // 2) + (0 if span == cut // 2 else side * span)
            columns = pl.ds(start if span == cut // 2 else pl.multiple_of(start, span), span)
            pay[far, :, width + j * span : width + (j + 1) * span] = gbuf[(j // 2) * chips + to, :, columns]
    total = product_in(gbuf, obuf, o)
    slope.wait()
    head = (total * sbuf[...]).astype(BF16)
    for far, out in enumerate(outs):
        pay[far, :, :width] = head
        leaving.start(pay.at[far], out)
    if with_parts:
        product_out(head, vbuf, v, stage, part_ref, leaving)
    leaving.wait()


def reduce_kernel(spread, deps, ids, got_ref, base_ref, *refs):
    out_ref, got, base, stage, sems, out_sems = refs[deps:]
    cuts, cut = got.shape[0], got.shape[-1]
    arriving, leaving = Copies(sems), Copies(out_sems)
    arriving.start(rows_place(base_ref, cut, ids[CORE])(ids[TP]), base)
    for i in range(4):
        some = pl.ds(i * (cuts // 4), cuts // 4)
        arriving.start(got_ref.at[some], got.at[some])
    arriving.wait()
    total = got[0].astype(F32)
    for i in range(1, cuts):
        total += got[i].astype(F32)
    stage[...] = (base[...].astype(F32) + total).astype(BF16)
    for i in range(cuts if spread else 1):
        leaving.start(stage, out_ref.at[i] if spread else out_ref)
    leaving.wait()


def settle_kernel(layer, ids, section_map, kept_ref, came_ref, out_ref, stage, sems, out_sems):
    rep = ids[REP]
    moved = section_map[rep, layer] // 2 > section_map[rep, layer - 1] // 2
    arriving, leaving = Copies(sems), Copies(out_sems)
    arriving.either(moved, came_ref, kept_ref, stage)
    arriving.wait()
    for i in range(out_ref.shape[0]):
        leaving.start(stage, out_ref.at[i])
    leaving.wait()


def carve_kernel(chips, ids, act_mine, act_sib, x_mine, x_sib, *refs):
    outs, sems = refs[:chips], refs[chips]
    chip, core = ids[CHIP], ids[CORE]
    width = act_mine.shape[-1]
    copies = []
    for k, (act, x) in enumerate(((act_mine, x_mine), (act_sib, x_sib))):
        at = core if k == 0 else 1 - core
        for far, out in enumerate(outs):
            to = lax.rem(chip + far, chips)
            for j, source in enumerate((act, x.at[to])):
                target = out.at[at, :, pl.ds(j * width, width)]
                copies.append(pltpu.make_async_copy(source, target, sems.at[k, far, j]))
                copies[-1].start()
    for copy in copies:
        copy.wait()


def pick_kernel(wanted, of_slots, deps, ids, section_map, *refs):
    chips = 4
    count = len(wanted)
    total = (2 if of_slots else count) * chips
    sources, (own_out, sib_out, rep_out, block, in_sems, sems) = refs[:total], refs[total + deps :]
    core, rep = ids[CORE], ids[REP]
    width = 2 * sib_out.shape[-1] - rep_out.shape[-1]
    span = rep_out.shape[-1] - sib_out.shape[-1]
    for n, layer in enumerate(wanted):
        section_core, slot, far = held_at(ids, section_map, layer)
        at = slot * chips + far if of_slots else n * chips + far
        for j in range(total) if of_slots else range(n * chips, (n + 1) * chips):

            def begin(n=n, j=j, section_core=section_core):
                source = sources[j].at[section_core] if of_slots else sources[j]
                pltpu.make_async_copy(source, block.at[n], in_sems.at[n]).start()

            pl.when(at == j)(begin)
    plan = ((own_out, [(rep, core)]), (sib_out, [(rep, 1 - core)]), (rep_out, [(1 - rep, core), (1 - rep, 1 - core)]))
    leaving = Copies(sems)
    for n in range(count):
        pltpu.make_async_copy(block.at[n], block.at[n], in_sems.at[n]).wait()
        for out, pieces in plan:
            leaving.start(block.at[n, :, pl.ds(0, width)], out.at[n, :, pl.ds(0, width)])
            for j, (replica, side) in enumerate(pieces):
                columns = pl.ds(pl.multiple_of(width + (replica * 2 + side) * span, span), span)
                leaving.start(block.at[n, :, columns], out.at[n, :, pl.ds(width + j * span, span)])
    leaving.wait()


def halves_kernel(starts, *refs):
    parts, (out_ref, sems) = refs[:4], refs[4:]
    arriving = Copies(sems)
    for k in range(4):
        arriving.start(parts[k].at[:, :, pl.ds(starts[k], out_ref.shape[-1])], out_ref.at[k])
    arriving.wait()


def gradient_kernel(whole, ids, *refs):
    value_ref, out_ref = refs[-2:]
    width = value_ref.shape[-1]
    first_side = ids[SIDE] == 0

    def factors(parts, mine=None, theirs=None):
        wide = jnp.concatenate([part[0][:, :width] for part in parts], axis=0)
        if mine is None:
            span = parts[0].shape[-1] - width
            starts = (width, width, width, width + span)
            return jnp.concatenate([p[0][:, i : i + span] for p, i in zip(parts, starts)], axis=0), wide
        mine, theirs = (jnp.concatenate([ref[k, 0] for k in range(4)], axis=0) for ref in (mine, theirs))
        left = jnp.where(first_side, mine, theirs)
        right = jnp.where(first_side, theirs, mine)
        return jnp.concatenate([left, right], axis=1), wide

    x, act = factors(refs[0:4], refs[4], refs[5])
    g, head = factors(refs[6:10]) if whole else factors(refs[6:10], refs[10], refs[11])
    value_ref[0] = lax.dot_general(x, head, TN, preferred_element_type=F32).astype(BF16)
    out_ref[0] = lax.dot_general(g, act, TN, preferred_element_type=F32).astype(BF16)


def gradients(ids, layers, first, count, forward, backward, before):
    quarter = forward[4].shape[-1]
    piece, width = 2 * quarter, forward[0].shape[-1] - quarter
    out = jax.ShapeDtypeStruct((layers, piece, width), BF16)
    out_spec = pl.BlockSpec((1, piece, width), lambda l: (first + l, 0, 0))

    def block(array, start):
        if array.ndim == 3:
            return pl.BlockSpec((1,) + array.shape[1:], lambda l: (start + l, 0, 0))
        return pl.BlockSpec((array.shape[0], 1) + array.shape[2:], lambda l: (0, start + l, 0, 0))

    specs = [SMEM] + [block(a, first) for a in forward] + [block(a, 0) for a in backward]
    operands = [ids] + list(forward) + list(backward)
    aliases = {}
    if before is not None:
        aliases = {len(operands): 0, len(operands) + 1: 1}
        operands, specs = operands + list(before), specs + [ANY, ANY]
    return pl.pallas_call(
        functools.partial(gradient_kernel, len(backward) == 4),
        out_shape=(out, out),
        grid=(count,),
        in_specs=specs,
        out_specs=(out_spec, out_spec),
        input_output_aliases=aliases,
        compiler_params=pltpu.CompilerParams(vmem_limit_bytes=VMEM_BYTES),
        cost_estimate=pl.CostEstimate(
            flops=count * 4 * piece * width * 256, bytes_accessed=count * 2400000, transcendentals=0
        ),
    )(*operands)


def per_device(section_map, checkpoint, top_grad, value_weight, out_weight):
    tp_total = lax.axis_size("tp")
    section_total = lax.axis_size("section")
    replica_total = lax.axis_size("rep")
    chips = section_total // 2
    rep, section, tp = (lax.axis_index(name) for name in ("rep", "section", "tp"))
    chip, core, side = section // 2, section % 2, tp % 2
    layers = section_map.shape[1]
    _, _, micro, tokens, model = checkpoint.shape
    slots, width = value_weight.shape[1], value_weight.shape[3]
    rows = micro * tokens
    cut = model // tp_total
    piece = model // (replica_total * section_total)
    v_own, o_own = value_weight[0], out_weight[0]
    x_pair, top_pair = checkpoint[0, 0], top_grad[0]

    ids = jnp.stack([rep, chip, core, side, tp]).astype(jnp.int32)

    chip_of = section_map // 2
    moves = chip_of[:, 1:] - chip_of[:, :-1]
    most_moves = jnp.max(moves, axis=0)

    swap = [(i, i ^ 1) for i in range(section_total)]

    def to_sibling(array):
        return lax.ppermute(array, "section", swap)

    def to_replica(array):
        return lax.ppermute(array, "rep", [(0, 1), (1, 0)])

    o_sib, v_sib = to_sibling(o_own), to_sibling(v_own)

    def shape(*dims, dtype=BF16):
        return jax.ShapeDtypeStruct(dims, dtype)

    def in_hbm(*dims):
        return pltpu.HBM(dims, BF16)

    def dma(*dims):
        return pltpu.SemaphoreType.DMA(dims)

    weight_bytes = model * width * 2
    weight_buffer = pltpu.VMEM((model, width), BF16)

    def reduce_slices(got, base, spread, *deps):
        count = got.shape[1]
        buffer = pltpu.VMEM((count, cut), BF16)
        return run(
            functools.partial(reduce_kernel, spread, len(deps)),
            (ids, got, base, *deps),
            [SMEM] + [ANY] * (2 + len(deps)),
            in_hbm(*got.shape) if spread else in_hbm(count, cut),
            HBM,
            [pltpu.VMEM(got.shape, BF16), buffer, buffer, dma(5), dma(tp_total if spread else 1)],
            got.size * 2,
        )

    def over_tp(parts):
        return lax.all_to_all(parts, "tp", 0, 0, tiled=True)

    def recompute_slot(slot, x, with_parts, deps=()):
        halves = (shape(tokens, width),) * 2 + (shape(tokens, width, dtype=F32),) * 2
        halves += (shape(chips, tokens, cut),) * 2
        outs = ((in_hbm(tp_total, rows, cut),) if with_parts else ()) + halves
        out_specs = ((HBM,) if with_parts else ()) + (VMEM,) * 6
        scratch = [pltpu.VMEM((tp_total, rows, cut), BF16), weight_buffer]
        scratch += [pltpu.VMEM((rows, width), BF16), pltpu.VMEM((rows, width), F32), dma(tp_total + 4), dma(2)]
        if with_parts:
            scratch += [weight_buffer, pltpu.VMEM((tp_total, rows, cut), BF16)]
        operands = (ids, x, v_own) + ((o_own,) if with_parts else ()) + tuple(deps)
        count = 2 if with_parts else 1
        return run(
            functools.partial(recompute, chips, with_parts, slot, len(deps)),
            operands,
            [SMEM] + [ANY] * (len(operands) - 1),
            outs,
            out_specs,
            scratch,
            count * weight_bytes,
            count * 2 * rows * model * width,
        )

    def along_chips(cuts):
        got = [cuts[0]]
        for far in range(1, chips):
            back = chips - far
            route = [(i, (i + 2 * back) % section_total) for i in range(section_total)]
            got.append(lax.ppermute(cuts[back], "section", route))
        return got

    def carve(act_mine, act_sib, x_mine, x_sib):
        block = in_hbm(2, tokens, width + cut)
        return run(
            functools.partial(carve_kernel, chips),
            (ids, act_mine, act_sib, x_mine, x_sib),
            [SMEM] + [VMEM] * 4,
            (block,) * chips,
            (HBM,) * chips,
            [dma(2, chips, 2)],
            2 * chips * tokens * (width + cut) * 4,
        )

    def to_owners(sources, wanted, of_slots, deps=(), later=None):
        count = len(wanted)
        columns = sources[0].shape[-1]
        span = (columns - width) // 4
        alone, both = in_hbm(count, tokens, width + span), in_hbm(count, tokens, width + 2 * span)
        own_out, sib_out, rep_out = run(
            functools.partial(pick_kernel, wanted, of_slots, len(deps)),
            (ids, section_map, *sources, *deps),
            [SMEM, SMEM] + [ANY] * (len(sources) + len(deps)),
            (alone, alone, both),
            (HBM,) * 3,
            [pltpu.VMEM((count, tokens, columns), BF16), dma(count), dma(7 * count)],
            count * tokens * columns * 6,
        )
        from_rep = to_replica(rep_out)
        if later is not None:
            from_rep, later = lax.optimization_barrier((from_rep, later))
        parts = (own_out, to_sibling(sib_out), from_rep, to_sibling(from_rep))
        if span == piece:
            return parts, later
        mine = run(
            functools.partial(halves_kernel, (width, width, width, width + span)),
            parts,
            [ANY] * 4,
            shape(4, count, tokens, span),
            VMEM,
            [dma(4)],
            16 * count * tokens * span,
        )
        theirs = lax.ppermute(mine, "tp", [(i, i ^ 1) for i in range(tp_total)])
        return parts + (mine, theirs)

    x_rows = x_pair.reshape(rows, model)
    parts, act_mine_0, act_other_0, slope_mine_0, slope_other_0, x_mine_0, x_other_0 = recompute_slot(0, x_rows, True)
    act_sib_0, slope_sib_0, x_sib_0 = to_sibling(act_other_0), to_sibling(slope_other_0), to_sibling(x_other_0)
    first_cuts = carve(act_mine_0, act_sib_0, x_mine_0, x_sib_0)
    first_got = along_chips(first_cuts)
    x_second = over_tp(reduce_slices(over_tp(parts), x_rows, True))
    act_mine_1, act_other_1, slope_mine_1, slope_other_1, x_mine_1, x_other_1 = recompute_slot(
        1, x_second, False, first_cuts
    )
    slope_sib_1, act_sib_1, x_sib_1 = to_sibling(slope_other_1), to_sibling(act_other_1), to_sibling(x_other_1)
    second_cuts = carve(act_mine_1, act_sib_1, x_mine_1, x_sib_1)
    second_got = along_chips(second_cuts)
    slopes = (slope_mine_0, slope_mine_1, slope_sib_0, slope_sib_1)

    down = [(i, i - 2) for i in range(2, section_total)]
    earlier, latest = [2, 3, 4, 5, 6, 7], [0, 1]

    def one_layer(layer, g, deps):
        last = layer == 0
        operands = (ids, section_map, g, *slopes, o_own, o_sib)
        operands += (() if last else (v_own, v_sib)) + tuple(deps)
        columns = width + (2 * cut if layer in latest else cut)
        block = in_hbm(tokens, columns)
        outs = (() if last else (in_hbm(tp_total, tokens, cut),)) + (block,) * chips
        scratch = [pltpu.VMEM((tp_total, tokens, cut), BF16), pltpu.VMEM((tokens, width), F32), weight_buffer]
        scratch += [pltpu.VMEM((chips, tokens, columns), BF16), dma(tp_total + 5), dma(chips + 2)]
        if not last:
            scratch += [weight_buffer, pltpu.VMEM((tp_total, tokens, cut), BF16)]
        count = 1 if last else 2
        result = run(
            functools.partial(step, chips, layer, len(deps)),
            operands,
            [SMEM, SMEM] + [ANY] * (len(operands) - 2),
            outs,
            (HBM,) * len(outs),
            scratch,
            count * weight_bytes,
            count * 2 * tokens * model * width,
        )
        return (None if last else result[0]), along_chips(result[-chips:])

    g = top_pair
    got_at = [None] * layers
    deps = {layer: [] for layer in range(layers)}

    def collect(wanted, deps=(), later=None):
        return to_owners([array for layer in wanted for array in got_at[layer]], wanted, False, deps, later)

    for layer in reversed(range(layers)):
        if layer == 7:
            deps[7] += first_got
        if layer == 6:
            deps[6] += list(second_cuts) + got_at[7][2:3]
        if layer == 5:
            deps[5] += second_got[1::2]
        if layer == 4:
            deps[4] += second_got[2:3] + got_at[6][2:3]
        if layer == 3:
            deps[3] += list(forward[:1])
        if layer == 2:
            deps[2] += got_at[3][2:3]
        if layer == 1:
            deps[1] += list(forward[:4])
        if layer == 0:
            deps[0] += got_at[1][2:3] + list(earlier_all[:4])
        parts, got_at[layer] = one_layer(layer, g, deps[layer])
        if layer == 0:
            break
        got = over_tp(parts)
        most = most_moves[layer - 1]

        def stay(*operands):
            return reduce_slices(*operands[:2], True, *operands[2:])

        def settle(kept, came, layer=layer):
            return run(
                functools.partial(settle_kernel, layer),
                (ids, section_map, kept, came),
                [SMEM, SMEM, ANY, ANY],
                in_hbm(tp_total, tokens, cut),
                HBM,
                [pltpu.VMEM((tokens, cut), BF16), dma(1), dma(tp_total)],
                tp_total * tokens * cut * 2,
            )

        def go_one(*operands):
            mine = reduce_slices(*operands[:2], False, *operands[2:])
            return settle(mine, lax.ppermute(mine, "section", down))

        def go_far(*operands, layer=layer, most=most):
            mine = reduce_slices(*operands[:2], False, *operands[2:])
            my_move = lax.dynamic_index_in_dim(moves, rep, 0, keepdims=False)[layer - 1]

            def hop(i, value):
                came = lax.ppermute(value, "section", down)
                return jnp.where(i < my_move, came, value)

            mine = lax.fori_loop(0, most, hop, mine)
            return settle(mine, mine)

        near = got_at[layer][1:] if layer in (5, 4, 2) else got_at[layer][1::2]
        spread = lax.switch(jnp.minimum(most, 2), (stay, go_one, go_far), got, g, *near)
        g = over_tp(spread)
        if layer == 4:
            forward = to_owners(first_got + second_got, list(range(layers)), True, (spread,))
        if layer == 2:
            earlier_all = collect(earlier, (spread,))

    result = gradients(ids, layers, earlier[0], len(earlier), forward, earlier_all, None)
    latest_all, result = collect(latest, (), result)
    return gradients(ids, layers, latest[0], len(latest), forward, latest_all, result)


def solution(mesh):
    placed = (
        P(),
        P("rep", "section", None, None, None),
        P("rep", None, None, None),
        P("rep", "section", None, "tp"),
        P("rep", "section", None, "tp"),
    )
    return jax.shard_map(
        per_device,
        mesh=mesh,
        in_specs=placed,
        out_specs=(P(None, ("rep", "section"), "tp"), P(None, ("rep", "section"), "tp")),
        check_vma=False,
    )
```

profile of v0, /device:TPU:1, one launch (start us, length us, event | category | flops | bytes accessed | tf_op | source)
XLA Modules:
  0.0 399.0 jit_solution(16536975212763550037)
XLA Ops:
  2.8 7.6 %shard_map.68 = (bf16[8,128,512]{2,1,0:T(8,128)(2,1)}, bf16[64,512]{1,0:T(8,128)(2,1)}, bf16[64,512]{1,0:T(8,128)(2,1)}, f32[64,512]{1,0:T(8,128)}, f32[64,512]{...) custom-call(s32[5]{0:T(128)} %stack.23.ids, bf16[128,4096]{1,0:T(8,128)(2,1)} %bitcast.48, ...), custom_call_target="tpu_custom_call" | custom-call | flops 1073741824 | bytes 8388608 | tf_op jit(solution)/shard_map/pallas_call | solution.py:39
  10.4 19.9 %all_to_all.80.got_ref = bf16[8,128,512]{2,1,0:T(8,128)(2,1)} all-to-all(bf16[8,128,512]{2,1,0:T(8,128)(2,1)} %get-tuple-element.720), channel_id=1, replica_groups=mesh['rep'=2,'section'=8,'tp'=8] {'tp'}, dimensions={0} | all-to-all | bytes 2097152 | tf_op jit(solution)/shard_map/all_to_all | solution.py:388
  62.1 6.3 %shard_map.73 = (bf16[8,64,512]{2,1,0:T(8,128)(2,1)}, bf16[64,1024]{1,0:T(8,128)(2,1)}, bf16[64,1024]{1,0:T(8,128)(2,1)}, bf16[64,1024]{1,0:T(8,128)(2,1)}, bf16[64,1024]{1,0:T(8,128)(2,1)}) custom-call(s32[5]{0:T(128)} %stack.23.ids, s32[2,8]{1,0:T(2,128)} %section_map.21, bf16[2,64,4096]{2,1,0:T(8,128)(2,1)} %bitcast.44, ...), custom_call_target="tpu_custom_call" | custom-call | flops 536870912 | bytes 8388608 | tf_op jit(solution)/shard_map/pallas_call | solution.py:39
  68.4 5.3 %all-to-all-start.2 = ((bf16[8,64,512]{2,1,0:T(8,128)(2,1)}), bf16[8,64,512]{2,1,0:T(8,128)(2,1)}, u32[]{:S(2)}, u32[]{:S(2)}) async-start(bf16[8,64,512]{2,1,0:T(8,128)(2,1)} %get-tuple-element.733), calls=%async_computation.2 | async-start | bytes 1048576 | tf_op jit(solution)/shard_map/all_to_all | solution.py:388
  98.6 6.2 %shard_map.74 = (bf16[8,64,512]{2,1,0:T(8,128)(2,1)}, bf16[64,1024]{1,0:T(8,128)(2,1)}, bf16[64,1024]{1,0:T(8,128)(2,1)}, bf16[64,1024]{1,0:T(8,128)(2,1)}, bf16[64,1024]{1,0:T(8,128)(2,1)}) custom-call(s32[5]{0:T(128)} %stack.23.ids, s32[2,8]{1,0:T(2,128)} %section_map.21, bf16[8,64,512]{2,1,0:T(8,128)(2,1)} %all-to-all-done.3.g_ref, ...), custom_call_target="tpu_custom_call" | custom-call | flops 536870912 | bytes 8388608 | tf_op jit(solution)/shard_map/pallas_call | solution.py:39
  104.8 5.5 %all-to-all-start.4 = ((bf16[8,64,512]{2,1,0:T(8,128)(2,1)}), bf16[8,64,512]{2,1,0:T(8,128)(2,1)}, u32[]{:S(2)}, u32[]{:S(2)}) async-start(bf16[8,64,512]{2,1,0:T(8,128)(2,1)} %get-tuple-element.737), calls=%async_computation.4 | async-start | bytes 1048576 | tf_op jit(solution)/shard_map/all_to_all | solution.py:388
  119.1 10.3 %conditional.8 = (bf16[8,64,512]{2,1,0:T(8,128)(2,1)}) conditional(s32[]{:T(128)} %clamp.23, (s32[5]{0:T(128)}, bf16[8,64,512]{2,1,0:T(8,128)(2,1)}, bf16[8,64,512]{2,1,0:T(8,128)(2,1)}, bf16[64,1024]{1,0:T(8,128)(2,1)}, bf16[64,1024]{1,0:T(8,128)(2,1)}) %tuple.102, (s32[5]{0:T(128)}, bf16[8,64,512]{2,1,0:T(8,128)(2,1)}, ...), branch_computations={%region_6.7_spmd, %region_7.8_spmd, %region_8.11_spmd} | conditional | flops 32774 | bytes 1507605 | solution.py:565
  140.7 6.2 %shard_map.75 = (bf16[8,64,512]{2,1,0:T(8,128)(2,1)}, bf16[64,1024]{1,0:T(8,128)(2,1)}, bf16[64,1024]{1,0:T(8,128)(2,1)}, bf16[64,1024]{1,0:T(8,128)(2,1)}, bf16[64,1024]{1,0:T(8,128)(2,1)}) custom-call(s32[5]{0:T(128)} %stack.23.ids, s32[2,8]{1,0:T(2,128)} %section_map.21, bf16[8,64,512]{2,1,0:T(8,128)(2,1)} %all-to-all-done.5.g_ref, ...), custom_call_target="tpu_custom_call" | custom-call | flops 536870912 | bytes 8388608 | tf_op jit(solution)/shard_map/pallas_call | solution.py:39
  159.2 10.3 %conditional.9 = (bf16[8,64,512]{2,1,0:T(8,128)(2,1)}) conditional(s32[]{:T(128)} %clamp.22, (s32[5]{0:T(128)}, bf16[8,64,512]{2,1,0:T(8,128)(2,1)}, bf16[8,64,512]{2,1,0:T(8,128)(2,1)}, bf16[64,1024]{1,0:T(8,128)(2,1)}, bf16[64,1024]{1,0:T(8,128)(2,1)}, /*index=5*/bf16[64,1024]{1,0:T(8,128)(2,1)}) %tuple.105, (s32[5]{0:T(128)}, ...), branch_computations={%region_11.12_spmd, %region_12.13_spmd, %region_13.16_spmd} | conditional | flops 32774 | bytes 1507605 | solution.py:565
  169.5 5.4 %all-to-all-start.7 = ((bf16[8,64,512]{2,1,0:T(8,128)(2,1)}), bf16[8,64,512]{2,1,0:T(8,128)(2,1)}, u32[]{:S(2)}, u32[]{:S(2)}) async-start(bf16[8,64,512]{2,1,0:T(8,128)(2,1)} %get-tuple-element.1140), calls=%async_computation.7 | async-start | bytes 1048576 | tf_op jit(solution)/shard_map/all_to_all | solution.py:388
  183.4 6.2 %shard_map.76 = (bf16[8,64,512]{2,1,0:T(8,128)(2,1)}, bf16[64,1024]{1,0:T(8,128)(2,1)}, bf16[64,1024]{1,0:T(8,128)(2,1)}, bf16[64,1024]{1,0:T(8,128)(2,1)}, bf16[64,1024]{1,0:T(8,128)(2,1)}) custom-call(s32[5]{0:T(128)} %stack.23.ids, s32[2,8]{1,0:T(2,128)} %section_map.21, bf16[8,64,512]{2,1,0:T(8,128)(2,1)} %all-to-all-done.7.g_ref, ...), custom_call_target="tpu_custom_call" | custom-call | flops 536870912 | bytes 8388608 | tf_op jit(solution)/shard_map/pallas_call | solution.py:39
  189.6 5.2 %all-to-all-start.8 = ((bf16[8,64,512]{2,1,0:T(8,128)(2,1)}), bf16[8,64,512]{2,1,0:T(8,128)(2,1)}, u32[]{:S(2)}, u32[]{:S(2)}) async-start(bf16[8,64,512]{2,1,0:T(8,128)(2,1)} %get-tuple-element.745), calls=%async_computation.8 | async-start | bytes 1048576 | tf_op jit(solution)/shard_map/all_to_all | solution.py:388
  202.1 11.4 %conditional.10 = (bf16[8,64,512]{2,1,0:T(8,128)(2,1)}) conditional(s32[]{:T(128)} %clamp.21, (s32[5]{0:T(128)}, bf16[8,64,512]{2,1,0:T(8,128)(2,1)}, bf16[8,64,512]{2,1,0:T(8,128)(2,1)}, bf16[64,1024]{1,0:T(8,128)(2,1)}, bf16[64,1024]{1,0:T(8,128)(2,1)}, /*index=5*/bf16[64,1024]{1,0:T(8,128)(2,1)}) %tuple.108, (s32[5]{0:T(128)}, ...), branch_computations={%region_16.17_spmd, %region_17.18_spmd, %region_18.21_spmd} | conditional | flops 32774 | bytes 1507605 | solution.py:565
  206.0 5.1 %collective-permute-done.3.came_ref = bf16[64,512]{1,0:T(8,128)(2,1)} collective-permute-done((bf16[64,512]{1,0:T(8,128)(2,1)}, bf16[64,512]{1,0:T(8,128)(2,1)}, u32[]{:S(2)}, u32[]{:S(2)}) %collective-permute-start.3) | collective-permute-done | bytes 65568 | tf_op jit(solution)/shard_map/cond/branch_1_fun/ppermute | solution.py:551
  213.5 5.0 %all-to-all-start.9 = ((bf16[8,64,512]{2,1,0:T(8,128)(2,1)}), bf16[8,64,512]{2,1,0:T(8,128)(2,1)}, u32[]{:S(2)}, u32[]{:S(2)}) async-start(bf16[8,64,512]{2,1,0:T(8,128)(2,1)} %get-tuple-element.1141.refs_8_), calls=%async_computation.9 | async-start | bytes 1048576 | tf_op jit(solution)/shard_map/all_to_all | solution.py:388
  225.7 6.1 %shard_map.79 = (bf16[8,64,512]{2,1,0:T(8,128)(2,1)}, bf16[64,1024]{1,0:T(8,128)(2,1)}, bf16[64,1024]{1,0:T(8,128)(2,1)}, bf16[64,1024]{1,0:T(8,128)(2,1)}, bf16[64,1024]{1,0:T(8,128)(2,1)}) custom-call(s32[5]{0:T(128)} %stack.23.ids, s32[2,8]{1,0:T(2,128)} %section_map.21, bf16[8,64,512]{2,1,0:T(8,128)(2,1)} %all-to-all-done.9.g_ref, ...), custom_call_target="tpu_custom_call" | custom-call | flops 536870912 | bytes 8388608 | tf_op jit(solution)/shard_map/pallas_call | solution.py:39
  244.7 11.9 %conditional.11 = (bf16[8,64,512]{2,1,0:T(8,128)(2,1)}) conditional(s32[]{:T(128)} %clamp.27, (s32[5]{0:T(128)}, bf16[8,64,512]{2,1,0:T(8,128)(2,1)}, bf16[8,64,512]{2,1,0:T(8,128)(2,1)}, bf16[64,1024]{1,0:T(8,128)(2,1)}, bf16[64,1024]{1,0:T(8,128)(2,1)}) %tuple.111, (s32[5]{0:T(128)}, bf16[8,64,512]{2,1,0:T(8,128)(2,1)}, ...), branch_computations={%region_21.22_spmd, %region_22.23_spmd, %region_23.26_spmd} | conditional | flops 32774 | bytes 1507605 | solution.py:565
  261.6 5.4 %collective-permute-done.46.refs_8_.refs_6_ = bf16[64,1024]{1,0:T(8,128)(2,1)} collective-permute-done((bf16[64,1024]{1,0:T(8,128)(2,1)}, bf16[64,1024]{1,0:T(8,128)(2,1)}, u32[]{:S(2)}, u32[]{:S(2)}) %collective-permute-start.46) | collective-permute-done | bytes 131104 | tf_op jit(solution)/shard_map/ppermute | solution.py:417
  268.2 6.1 %shard_map.80 = (bf16[8,64,512]{2,1,0:T(8,128)(2,1)}, bf16[64,1024]{1,0:T(8,128)(2,1)}, bf16[64,1024]{1,0:T(8,128)(2,1)}, bf16[64,1024]{1,0:T(8,128)(2,1)}, bf16[64,1024]{1,0:T(8,128)(2,1)}) custom-call(s32[5]{0:T(128)} %stack.23.ids, s32[2,8]{1,0:T(2,128)} %section_map.21, bf16[8,64,512]{2,1,0:T(8,128)(2,1)} %all-to-all-done.11.g_ref, ...), custom_call_target="tpu_custom_call" | custom-call | flops 536870912 | bytes 8388608 | tf_op jit(solution)/shard_map/pallas_call | solution.py:39
  278.5 17.2 %collective-permute-start.42 = (bf16[8,64,768]{2,1,0:T(8,128)(2,1)}, bf16[8,64,768]{2,1,0:T(8,128)(2,1)}, u32[]{:S(2)}, u32[]{:S(2)}) collective-permute-start(bf16[8,64,768]{2,1,0:T(8,128)(2,1)} %collective-permute-done.41.refs_2_.refs_10_), channel_id=1, source_target_pairs={{0,8},{8,0},{16,24},{24,16},{32,40},{40,32},{48,56},{56,48},{1,9},... | collective-permute-start | bytes 2359304 | tf_op jit(solution)/shard_map/ppermute | solution.py:355
  306.5 10.3 %conditional.12 = (bf16[8,64,512]{2,1,0:T(8,128)(2,1)}) conditional(s32[]{:T(128)} %clamp.26, (s32[5]{0:T(128)}, bf16[8,64,512]{2,1,0:T(8,128)(2,1)}, bf16[8,64,512]{2,1,0:T(8,128)(2,1)}, bf16[64,1024]{1,0:T(8,128)(2,1)}, bf16[64,1024]{1,0:T(8,128)(2,1)}, /*index=5*/bf16[64,1024]{1,0:T(8,128)(2,1)}) %tuple.114, (s32[5]{0:T(128)}, ...), branch_computations={%region_26.27_spmd, %region_27.28_spmd, %region_28.31_spmd} | conditional | flops 32774 | bytes 1507605 | solution.py:565
  316.9 5.2 %all-to-all-start.13 = ((bf16[8,64,512]{2,1,0:T(8,128)(2,1)}), bf16[8,64,512]{2,1,0:T(8,128)(2,1)}, u32[]{:S(2)}, u32[]{:S(2)}) async-start(bf16[8,64,512]{2,1,0:T(8,128)(2,1)} %get-tuple-element.1143.refs_24_), calls=%async_computation.13 | async-start | bytes 1048576 | tf_op jit(solution)/shard_map/all_to_all | solution.py:388
  329.3 6.2 %shard_map.81 = (bf16[8,64,512]{2,1,0:T(8,128)(2,1)}, bf16[64,1536]{1,0:T(8,128)(2,1)}, bf16[64,1536]{1,0:T(8,128)(2,1)}, bf16[64,1536]{1,0:T(8,128)(2,1)}, bf16[64,1536]{1,0:T(8,128)(2,1)}) custom-call(s32[5]{0:T(128)} %stack.23.ids, s32[2,8]{1,0:T(2,128)} %section_map.21, bf16[8,64,512]{2,1,0:T(8,128)(2,1)} %all-to-all-done.13.g_ref, ...), custom_call_target="tpu_custom_call" | custom-call | flops 536870912 | bytes 8388608 | tf_op jit(solution)/shard_map/pallas_call | solution.py:39
  383.3 6.5 %shard_map.86 = (bf16[8,256,512]{2,1,0:T(8,128)(2,1)}, bf16[8,256,512]{2,1,0:T(8,128)(2,1)}) custom-call(s32[5]{0:T(128)} %stack.23.ids, bf16[8,64,640]{2,1,0:T(8,128)(2,1)} %get-tuple-element.749.refs_0_.refs_8_, bf16[8,64,640]{2,1,0:T(8,128)(2,1)} %collective-permute-done.40.refs_1_.refs_9_, bf16[8,64,768]{2,1,0:T(8,128)(2,1)} %collective-permute-done.41.refs_2_.refs_10_, ...), custom_call_target="tpu_custom_call" | custom-call | flops 805306368 | bytes 14400000 | tf_op jit(solution)/shard_map/pallas_call | solution.py:316
  (155 shorter events, 253.2 us)
Async XLA Ops:
  0.6 61.4 %collective-permute-start.27 = (bf16[2,4096,512]{2,1,0:T(8,128)(2,1)}, bf16[2,4096,512]{2,1,0:T(8,128)(2,1)}, u32[]{:S(2)}, u32[]{:S(2)}) collective-permute-start(bf16[2,4096,512]{2,1,0:T(8,128)(2,1)} %bitcast.24), channel_id=1, source_target_pairs={{0,8},{8,0},{16,24},{24,16},{32,40},{40,32},{48,56},{56,48},{1,9},... | collective-permute-start | bytes 25165832 | tf_op jit(solution)/shard_map/ppermute | solution.py:355
  2.1 59.9 %collective-permute-start.26 = (bf16[2,4096,512]{2,1,0:T(8,128)(2,1)}, bf16[2,4096,512]{2,1,0:T(8,128)(2,1)}, u32[]{:S(2)}, u32[]{:S(2)}) collective-permute-start(bf16[2,4096,512]{2,1,0:T(8,128)(2,1)} %bitcast.34), channel_id=1, source_target_pairs={{0,8},{8,0},{16,24},{24,16},{32,40},{40,32},{48,56},{56,48},{1,9},... | collective-permute-start | bytes 25165832 | tf_op jit(solution)/shard_map/ppermute | solution.py:355
  33.5 18.2 %all-to-all-start.1 = ((bf16[8,128,512]{2,1,0:T(8,128)(2,1)}), bf16[8,128,512]{2,1,0:T(8,128)(2,1)}, u32[]{:S(2)}, u32[]{:S(2)}) async-start(bf16[8,128,512]{2,1,0:T(8,128)(2,1)} %shard_map.70), calls=%async_computation.1 | async-start | bytes 2097152 | tf_op jit(solution)/shard_map/all_to_all | solution.py:388
  43.8 13.7 %collective-permute-start.16 = (bf16[2,64,1024]{2,1,0:T(8,128)(2,1)}, bf16[2,64,1024]{2,1,0:T(8,128)(2,1)}, u32[]{:S(2)}, u32[]{:S(2)}) collective-permute-start(bf16[2,64,1024]{2,1,0:T(8,128)(2,1)} %get-tuple-element.717.refs_3_), channel_id=1, source_target_pairs={{0,48},{8,56},{16,0},{24,8},{32,16},{40,24},{48,32},{56,40},{1,49}... | collective-permute-start | bytes 786440 | tf_op jit(solution)/shard_map/ppermute | solution.py:417
  46.4 12.9 %collective-permute-start.17 = (bf16[2,64,1024]{2,1,0:T(8,128)(2,1)}, bf16[2,64,1024]{2,1,0:T(8,128)(2,1)}, u32[]{:S(2)}, u32[]{:S(2)}) collective-permute-start(bf16[2,64,1024]{2,1,0:T(8,128)(2,1)} %get-tuple-element.718.refs_2_), channel_id=1, source_target_pairs={{0,32},{8,40},{16,48},{24,56},{32,0},{40,8},{48,16},{56,24},{1,33}... | collective-permute-start | bytes 786440 | tf_op jit(solution)/shard_map/ppermute | solution.py:417
  46.9 15.1 %collective-permute-start.18 = (bf16[2,64,1024]{2,1,0:T(8,128)(2,1)}, bf16[2,64,1024]{2,1,0:T(8,128)(2,1)}, u32[]{:S(2)}, u32[]{:S(2)}) collective-permute-start(bf16[2,64,1024]{2,1,0:T(8,128)(2,1)} %get-tuple-element.719.refs_1_), channel_id=1, source_target_pairs={{0,16},{8,24},{16,32},{24,40},{32,48},{40,56},{48,0},{56,8},{1,17}... | collective-permute-start | bytes 786440 | tf_op jit(solution)/shard_map/ppermute | solution.py:417
  68.4 14.4 %all-to-all-start.2 = ((bf16[8,64,512]{2,1,0:T(8,128)(2,1)}), bf16[8,64,512]{2,1,0:T(8,128)(2,1)}, u32[]{:S(2)}, u32[]{:S(2)}) async-start(bf16[8,64,512]{2,1,0:T(8,128)(2,1)} %get-tuple-element.733), calls=%async_computation.2 | async-start | bytes 1048576 | tf_op jit(solution)/shard_map/all_to_all | solution.py:388
  85.6 13.0 %all-to-all-start.3 = ((bf16[8,64,512]{2,1,0:T(8,128)(2,1)}), bf16[8,64,512]{2,1,0:T(8,128)(2,1)}, u32[]{:S(2)}, u32[]{:S(2)}) async-start(bf16[8,64,512]{2,1,0:T(8,128)(2,1)} %get-tuple-element.1138), calls=%async_computation.3 | async-start | bytes 1048576 | tf_op jit(solution)/shard_map/all_to_all | solution.py:388
  104.8 14.3 %all-to-all-start.4 = ((bf16[8,64,512]{2,1,0:T(8,128)(2,1)}), bf16[8,64,512]{2,1,0:T(8,128)(2,1)}, u32[]{:S(2)}, u32[]{:S(2)}) async-start(bf16[8,64,512]{2,1,0:T(8,128)(2,1)} %get-tuple-element.737), calls=%async_computation.4 | async-start | bytes 1048576 | tf_op jit(solution)/shard_map/all_to_all | solution.py:388
  146.8 12.4 %all-to-all-start.6 = ((bf16[8,64,512]{2,1,0:T(8,128)(2,1)}), bf16[8,64,512]{2,1,0:T(8,128)(2,1)}, u32[]{:S(2)}, u32[]{:S(2)}) async-start(bf16[8,64,512]{2,1,0:T(8,128)(2,1)} %get-tuple-element.740), calls=%async_computation.6 | async-start | bytes 1048576 | tf_op jit(solution)/shard_map/all_to_all | solution.py:388
  169.5 13.9 %all-to-all-start.7 = ((bf16[8,64,512]{2,1,0:T(8,128)(2,1)}), bf16[8,64,512]{2,1,0:T(8,128)(2,1)}, u32[]{:S(2)}, u32[]{:S(2)}) async-start(bf16[8,64,512]{2,1,0:T(8,128)(2,1)} %get-tuple-element.1140), calls=%async_computation.7 | async-start | bytes 1048576 | tf_op jit(solution)/shard_map/all_to_all | solution.py:388
  189.6 12.5 %all-to-all-start.8 = ((bf16[8,64,512]{2,1,0:T(8,128)(2,1)}), bf16[8,64,512]{2,1,0:T(8,128)(2,1)}, u32[]{:S(2)}, u32[]{:S(2)}) async-start(bf16[8,64,512]{2,1,0:T(8,128)(2,1)} %get-tuple-element.745), calls=%async_computation.8 | async-start | bytes 1048576 | tf_op jit(solution)/shard_map/all_to_all | solution.py:388
  231.8 12.9 %all-to-all-start.10 = ((bf16[8,64,512]{2,1,0:T(8,128)(2,1)}), bf16[8,64,512]{2,1,0:T(8,128)(2,1)}, u32[]{:S(2)}, u32[]{:S(2)}) async-start(bf16[8,64,512]{2,1,0:T(8,128)(2,1)} %get-tuple-element.752), calls=%async_computation.10 | async-start | bytes 1048576 | tf_op jit(solution)/shard_map/all_to_all | solution.py:388
  236.0 42.5 %collective-permute-start.41 = (bf16[8,64,768]{2,1,0:T(8,128)(2,1)}, bf16[8,64,768]{2,1,0:T(8,128)(2,1)}, u32[]{:S(2)}, u32[]{:S(2)}) collective-permute-start(bf16[8,64,768]{2,1,0:T(8,128)(2,1)} %get-tuple-element.751), channel_id=1, source_target_pairs={{0,64},{64,0},{1,65},{65,1},{2,66},{66,2},{3,67},{67,3},{4,68},{68... | collective-permute-start | bytes 2359304 | tf_op jit(solution)/shard_map/ppermute | solution.py:358
  274.3 32.2 %all-to-all-start.12 = ((bf16[8,64,512]{2,1,0:T(8,128)(2,1)}), bf16[8,64,512]{2,1,0:T(8,128)(2,1)}, u32[]{:S(2)}, u32[]{:S(2)}) async-start(bf16[8,64,512]{2,1,0:T(8,128)(2,1)} %get-tuple-element.756), calls=%async_computation.12 | async-start | bytes 1048576 | tf_op jit(solution)/shard_map/all_to_all | solution.py:388
  278.5 47.6 %collective-permute-start.42 = (bf16[8,64,768]{2,1,0:T(8,128)(2,1)}, bf16[8,64,768]{2,1,0:T(8,128)(2,1)}, u32[]{:S(2)}, u32[]{:S(2)}) collective-permute-start(bf16[8,64,768]{2,1,0:T(8,128)(2,1)} %collective-permute-done.41.refs_2_.refs_10_), channel_id=1, source_target_pairs={{0,8},{8,0},{16,24},{24,16},{32,40},{40,32},{48,56},{56,48},{1,9},... | collective-permute-start | bytes 2359304 | tf_op jit(solution)/shard_map/ppermute | solution.py:355
  295.7 30.4 %collective-permute-start.40 = (bf16[8,64,640]{2,1,0:T(8,128)(2,1)}, bf16[8,64,640]{2,1,0:T(8,128)(2,1)}, u32[]{:S(2)}, u32[]{:S(2)}) collective-permute-start(bf16[8,64,640]{2,1,0:T(8,128)(2,1)} %get-tuple-element.750), channel_id=1, source_target_pairs={{0,8},{8,0},{16,24},{24,16},{32,40},{40,32},{48,56},{56,48},{1,9},... | collective-permute-start | bytes 1966088 | tf_op jit(solution)/shard_map/ppermute | solution.py:355
  316.9 12.4 %all-to-all-start.13 = ((bf16[8,64,512]{2,1,0:T(8,128)(2,1)}), bf16[8,64,512]{2,1,0:T(8,128)(2,1)}, u32[]{:S(2)}, u32[]{:S(2)}) async-start(bf16[8,64,512]{2,1,0:T(8,128)(2,1)} %get-tuple-element.1143.refs_24_), calls=%async_computation.13 | async-start | bytes 1048576 | tf_op jit(solution)/shard_map/all_to_all | solution.py:388
  325.2 17.4 %collective-permute-start.54 = (bf16[6,64,768]{2,1,0:T(8,128)(2,1)}, bf16[6,64,768]{2,1,0:T(8,128)(2,1)}, u32[]{:S(2)}, u32[]{:S(2)}) collective-permute-start(bf16[6,64,768]{2,1,0:T(8,128)(2,1)} %get-tuple-element.772), channel_id=1, source_target_pairs={{0,64},{64,0},{1,65},{65,1},{2,66},{66,2},{3,67},{67,3},{4,68},{68... | collective-permute-start | bytes 1769480 | tf_op jit(solution)/shard_map/ppermute | solution.py:358
  335.4 12.3 %all-to-all-start.14 = ((bf16[8,64,512]{2,1,0:T(8,128)(2,1)}), bf16[8,64,512]{2,1,0:T(8,128)(2,1)}, u32[]{:S(2)}, u32[]{:S(2)}) async-start(bf16[8,64,512]{2,1,0:T(8,128)(2,1)} %get-tuple-element.760), calls=%async_computation.14 | async-start | bytes 1048576 | tf_op jit(solution)/shard_map/all_to_all | solution.py:388
  342.6 17.4 %collective-permute-start.55 = (bf16[6,64,768]{2,1,0:T(8,128)(2,1)}, bf16[6,64,768]{2,1,0:T(8,128)(2,1)}, u32[]{:S(2)}, u32[]{:S(2)}) collective-permute-start(bf16[6,64,768]{2,1,0:T(8,128)(2,1)} %collective-permute-done.54.refs_9_.refs_2_.refs_8_), channel_id=1, source_target_pairs={{0,8},{8,0},{16,24},{24,16},{32,40},{40,32},{48,56},{56,48},{1,9},... | collective-permute-start | bytes 1769480 | tf_op jit(solution)/shard_map/ppermute | solution.py:355
  346.5 13.5 %collective-permute-start.53 = (bf16[6,64,640]{2,1,0:T(8,128)(2,1)}, bf16[6,64,640]{2,1,0:T(8,128)(2,1)}, u32[]{:S(2)}, u32[]{:S(2)}) collective-permute-start(bf16[6,64,640]{2,1,0:T(8,128)(2,1)} %get-tuple-element.771), channel_id=1, source_target_pairs={{0,8},{8,0},{16,24},{24,16},{32,40},{40,32},{48,56},{56,48},{1,9},... | collective-permute-start | bytes 1474568 | tf_op jit(solution)/shard_map/ppermute | solution.py:355
  358.6 23.0 %collective-permute-start.43 = (bf16[4,8,64,128]{3,2,1,0:T(8,128)(2,1)}, bf16[4,8,64,128]{3,2,1,0:T(8,128)(2,1)}, u32[]{:S(2)}, u32[]{:S(2)}) collective-permute-start(bf16[4,8,64,128]{3,2,1,0:T(8,128)(2,1)} %shard_map.78.refs_4_), channel_id=1, source_target_pairs={{0,1},{1,0},{2,3},{3,2},{4,5},{5,4},{6,7},{7,6},{8,9},{9,8},{10,11... | collective-permute-start | bytes 1572872 | tf_op jit(solution)/shard_map/ppermute | solution.py:461
  361.8 21.6 %collective-permute-start.61 = (bf16[4,6,64,128]{3,2,1,0:T(8,128)(2,1)}, bf16[4,6,64,128]{3,2,1,0:T(8,128)(2,1)}, u32[]{:S(2)}, u32[]{:S(2)}) collective-permute-start(bf16[4,6,64,128]{3,2,1,0:T(8,128)(2,1)} %shard_map.85.refs_10_), channel_id=1, source_target_pairs={{0,1},{1,0},{2,3},{3,2},{4,5},{5,4},{6,7},{7,6},{8,9},{9,8},{10,11... | collective-permute-start | bytes 1179656 | tf_op jit(solution)/shard_map/ppermute | solution.py:461
  (44 other events, 268.8 us)
where the time goes:
time: 401 us; the launch traced here: 399 us
  starting transfers between devices  144 us (36%)
  Pallas kernels  118 us (29%)
  waiting for transfers between devices  99.5 us (25%)
  blocking collectives  19.9 us (5%)
  loops' own time  9.27 us (2%)
  between operations  5.66 us (1%)
    pallas_call x29, Pallas kernels, run(): pl.pallas_call(kernel, out_shape=outs, in_specs=specs, out_specs=out_spec...  109 us
    all_to_all x15, starting transfers between devices, over_tp(): return lax.all_to_all(parts, 'tp', 0, 0, tiled=True)  70.4 us
    ppermute x30, waiting for transfers between devices, along_chips(): got.append(lax.ppermute(cuts[back], 'section', route))  57.6 us
    ppermute x14, starting transfers between devices, to_sibling(): return lax.ppermute(array, 'section', swap)  34 us
    ppermute x30, starting transfers between devices, along_chips(): got.append(lax.ppermute(cuts[back], 'section', route))  25.1 us
    all_to_all x1, blocking collectives, over_tp(): return lax.all_to_all(parts, 'tp', 0, 0, tiled=True)  19.9 us
    all_to_all x15, waiting for transfers between devices, over_tp(): return lax.all_to_all(parts, 'tp', 0, 0, tiled=True)  17.4 us
    ppermute x4, waiting for transfers between devices, go_one(): return settle(mine, lax.ppermute(mine, 'section', down))  17.2 us
  transfers between devices with their start and end apart: 68, of which 44 were waited for; matrix products, arithmetic and copies ran while one was open for 1% of the time, Pallas kernels for 17%

commit v1 on v0

--- a/solution.py
+++ b/solution.py
@@ -296,7 +296,7 @@
     out_ref[0] = lax.dot_general(g, act, TN, preferred_element_type=F32).astype(BF16)
 
 
-def gradients(ids, layers, first, count, forward, backward, before):
+def gradients(ids, layers, first, count, forward, backward, before, after=None):
     quarter = forward[4].shape[-1]
     piece, width = 2 * quarter, forward[0].shape[-1] - quarter
     out = jax.ShapeDtypeStruct((layers, piece, width), BF16)
@@ -313,6 +313,8 @@
     if before is not None:
         aliases = {len(operands): 0, len(operands) + 1: 1}
         operands, specs = operands + list(before), specs + [ANY, ANY]
+    if after is not None:
+        operands, specs = operands + [after], specs + [ANY]
     return pl.pallas_call(
         functools.partial(gradient_kernel, len(backward) == 4),
         out_shape=(out, out),
@@ -443,10 +445,10 @@
             [pltpu.VMEM((count, tokens, columns), BF16), dma(count), dma(7 * count)],
             count * tokens * columns * 6,
         )
-        from_rep = to_replica(rep_out)
+        from_rep, from_sib = to_replica(rep_out), to_sibling(sib_out)
         if later is not None:
-            from_rep, later = lax.optimization_barrier((from_rep, later))
-        parts = (own_out, to_sibling(sib_out), from_rep, to_sibling(from_rep))
+            from_rep, later = lax.optimization_barrier((from_rep, later(from_sib)))
+        parts = (own_out, from_sib, from_rep, to_sibling(from_rep))
         if span == piece:
             return parts, later
         mine = run(
@@ -569,8 +571,10 @@
         if layer == 2:
             earlier_all = collect(earlier, (spread,))
 
-    result = gradients(ids, layers, earlier[0], len(earlier), forward, earlier_all, None)
-    latest_all, result = collect(latest, (), result)
+    def earlier_gradients(after):
+        return gradients(ids, layers, earlier[0], len(earlier), forward, earlier_all, None, after)
+
+    latest_all, result = collect(latest, (), earlier_gradients)
     return gradients(ids, layers, latest[0], len(latest), forward, latest_all, result)
 
 

time: 401 us -> 407 us (1.015); the launches traced: 399 us -> 399 us
  transfers between devices with their start and end apart: 68 -> 68, of which waited for: 44 -> 46; matrix products, arithmetic and copies ran while one was open for 1% -> 1% of each run, Pallas kernels for 17% -> 17%
where the time goes in v1:
time: 407 us; the launch traced here: 399 us
  starting transfers between devices  147 us (36%)
  Pallas kernels  118 us (29%)
  waiting for transfers between devices  96.3 us (24%)
  blocking collectives  19.9 us (5%)
  loops' own time  9.27 us (2%)
  between operations  5.66 us (1%)
    pallas_call x29, Pallas kernels, run(): pl.pallas_call(kernel, out_shape=outs, in_specs=specs, out_specs=out_spec...  109 us
    all_to_all x15, starting transfers between devices, over_tp(): return lax.all_to_all(parts, 'tp', 0, 0, tiled=True)  70.3 us
    ppermute x30, waiting for transfers between devices, along_chips(): got.append(lax.ppermute(cuts[back], 'section', route))  54.1 us
    ppermute x14, starting transfers between devices, to_sibling(): return lax.ppermute(array, 'section', swap)  36.8 us
    ppermute x30, starting transfers between devices, along_chips(): got.append(lax.ppermute(cuts[back], 'section', route))  26.2 us
    all_to_all x1, blocking collectives, over_tp(): return lax.all_to_all(parts, 'tp', 0, 0, tiled=True)  19.9 us
    all_to_all x15, waiting for transfers between devices, over_tp(): return lax.all_to_all(parts, 'tp', 0, 0, tiled=True)  17.7 us
    ppermute x4, waiting for transfers between devices, go_one(): return settle(mine, lax.ppermute(mine, 'section', down))  16.5 us
  transfers between devices with their start and end apart: 68, of which 46 were waited for; matrix products, arithmetic and copies ran while one was open for 1% of the time, Pallas kernels for 17%

profile of v1, /device:TPU:1, one launch (start us, length us, event | category | flops | bytes accessed | tf_op | source)
XLA Modules:
  0.0 399.2 jit_solution(8628568000863860632)
XLA Ops:
  2.8 7.6 %shard_map.68 = (bf16[8,128,512]{2,1,0:T(8,128)(2,1)}, bf16[64,512]{1,0:T(8,128)(2,1)}, bf16[64,512]{1,0:T(8,128)(2,1)}, f32[64,512]{1,0:T(8,128)}, f32[64,512]{...) custom-call(s32[5]{0:T(128)} %stack.23.ids, bf16[128,4096]{1,0:T(8,128)(2,1)} %bitcast.48, ...), custom_call_target="tpu_custom_call" | custom-call | flops 1073741824 | bytes 8388608 | tf_op jit(solution)/shard_map/pallas_call | solution.py:39
  10.4 19.9 %all_to_all.80.got_ref = bf16[8,128,512]{2,1,0:T(8,128)(2,1)} all-to-all(bf16[8,128,512]{2,1,0:T(8,128)(2,1)} %get-tuple-element.720), channel_id=1, replica_groups=mesh['rep'=2,'section'=8,'tp'=8] {'tp'}, dimensions={0} | all-to-all | bytes 2097152 | tf_op jit(solution)/shard_map/all_to_all | solution.py:390
  51.7 4.9 %shard_map.71 = (bf16[64,512]{1,0:T(8,128)(2,1)}, bf16[64,512]{1,0:T(8,128)(2,1)}, f32[64,512]{1,0:T(8,128)}, f32[64,512]{1,0:T(8,128)}, bf16[4,64,512]{2,1,0:T(8,128)(2,1)}, /*index=5*/bf16[4,64,512]{2,1,0:T(8,128)(2,1)}) custom-call(s32[5]{0:T(128)} %stack.23.ids, bf16[8,128,512]{2,1,0:T(8,128)(2,1)} %all-to-all-done.1.x_ref, ...), custom_call_target="tpu_custom_call" | custom-call | flops 536870912 | bytes 4194304 | tf_op jit(solution)/shard_map/pallas_call | solution.py:39
  62.0 6.3 %shard_map.73 = (bf16[8,64,512]{2,1,0:T(8,128)(2,1)}, bf16[64,1024]{1,0:T(8,128)(2,1)}, bf16[64,1024]{1,0:T(8,128)(2,1)}, bf16[64,1024]{1,0:T(8,128)(2,1)}, bf16[64,1024]{1,0:T(8,128)(2,1)}) custom-call(s32[5]{0:T(128)} %stack.23.ids, s32[2,8]{1,0:T(2,128)} %section_map.21, bf16[2,64,4096]{2,1,0:T(8,128)(2,1)} %bitcast.44, ...), custom_call_target="tpu_custom_call" | custom-call | flops 536870912 | bytes 8388608 | tf_op jit(solution)/shard_map/pallas_call | solution.py:39
  68.3 5.3 %all-to-all-start.2 = ((bf16[8,64,512]{2,1,0:T(8,128)(2,1)}), bf16[8,64,512]{2,1,0:T(8,128)(2,1)}, u32[]{:S(2)}, u32[]{:S(2)}) async-start(bf16[8,64,512]{2,1,0:T(8,128)(2,1)} %get-tuple-element.733), calls=%async_computation.2 | async-start | bytes 1048576 | tf_op jit(solution)/shard_map/all_to_all | solution.py:390
  98.6 6.2 %shard_map.74 = (bf16[8,64,512]{2,1,0:T(8,128)(2,1)}, bf16[64,1024]{1,0:T(8,128)(2,1)}, bf16[64,1024]{1,0:T(8,128)(2,1)}, bf16[64,1024]{1,0:T(8,128)(2,1)}, bf16[64,1024]{1,0:T(8,128)(2,1)}) custom-call(s32[5]{0:T(128)} %stack.23.ids, s32[2,8]{1,0:T(2,128)} %section_map.21, bf16[8,64,512]{2,1,0:T(8,128)(2,1)} %all-to-all-done.3.g_ref, ...), custom_call_target="tpu_custom_call" | custom-call | flops 536870912 | bytes 8388608 | tf_op jit(solution)/shard_map/pallas_call | solution.py:39
  104.8 5.5 %all-to-all-start.4 = ((bf16[8,64,512]{2,1,0:T(8,128)(2,1)}), bf16[8,64,512]{2,1,0:T(8,128)(2,1)}, u32[]{:S(2)}, u32[]{:S(2)}) async-start(bf16[8,64,512]{2,1,0:T(8,128)(2,1)} %get-tuple-element.737), calls=%async_computation.4 | async-start | bytes 1048576 | tf_op jit(solution)/shard_map/all_to_all | solution.py:390
  119.1 10.3 %conditional.8 = (bf16[8,64,512]{2,1,0:T(8,128)(2,1)}) conditional(s32[]{:T(128)} %clamp.23, (s32[5]{0:T(128)}, bf16[8,64,512]{2,1,0:T(8,128)(2,1)}, bf16[8,64,512]{2,1,0:T(8,128)(2,1)}, bf16[64,1024]{1,0:T(8,128)(2,1)}, bf16[64,1024]{1,0:T(8,128)(2,1)}) %tuple.102, (s32[5]{0:T(128)}, bf16[8,64,512]{2,1,0:T(8,128)(2,1)}, ...), branch_computations={%region_6.7_spmd, %region_7.8_spmd, %region_8.11_spmd} | conditional | flops 32774 | bytes 1507597 | solution.py:567
  140.7 6.2 %shard_map.75 = (bf16[8,64,512]{2,1,0:T(8,128)(2,1)}, bf16[64,1024]{1,0:T(8,128)(2,1)}, bf16[64,1024]{1,0:T(8,128)(2,1)}, bf16[64,1024]{1,0:T(8,128)(2,1)}, bf16[64,1024]{1,0:T(8,128)(2,1)}) custom-call(s32[5]{0:T(128)} %stack.23.ids, s32[2,8]{1,0:T(2,128)} %section_map.21, bf16[8,64,512]{2,1,0:T(8,128)(2,1)} %all-to-all-done.5.g_ref, ...), custom_call_target="tpu_custom_call" | custom-call | flops 536870912 | bytes 8388608 | tf_op jit(solution)/shard_map/pallas_call | solution.py:39
  146.8 4.7 %all-to-all-start.6 = ((bf16[8,64,512]{2,1,0:T(8,128)(2,1)}), bf16[8,64,512]{2,1,0:T(8,128)(2,1)}, u32[]{:S(2)}, u32[]{:S(2)}) async-start(bf16[8,64,512]{2,1,0:T(8,128)(2,1)} %get-tuple-element.740), calls=%async_computation.6 | async-start | bytes 1048576 | tf_op jit(solution)/shard_map/all_to_all | solution.py:390
  162.0 5.4 %all-to-all-start.7 = ((bf16[8,64,512]{2,1,0:T(8,128)(2,1)}), bf16[8,64,512]{2,1,0:T(8,128)(2,1)}, u32[]{:S(2)}, u32[]{:S(2)}) async-start(bf16[8,64,512]{2,1,0:T(8,128)(2,1)} %get-tuple-element.1140), calls=%async_computation.7 | async-start | bytes 1048576 | tf_op jit(solution)/shard_map/all_to_all | solution.py:390
  175.9 6.2 %shard_map.76 = (bf16[8,64,512]{2,1,0:T(8,128)(2,1)}, bf16[64,1024]{1,0:T(8,128)(2,1)}, bf16[64,1024]{1,0:T(8,128)(2,1)}, bf16[64,1024]{1,0:T(8,128)(2,1)}, bf16[64,1024]{1,0:T(8,128)(2,1)}) custom-call(s32[5]{0:T(128)} %stack.23.ids, s32[2,8]{1,0:T(2,128)} %section_map.21, bf16[8,64,512]{2,1,0:T(8,128)(2,1)} %all-to-all-done.7.g_ref, ...), custom_call_target="tpu_custom_call" | custom-call | flops 536870912 | bytes 8388608 | tf_op jit(solution)/shard_map/pallas_call | solution.py:39
  182.1 5.2 %all-to-all-start.8 = ((bf16[8,64,512]{2,1,0:T(8,128)(2,1)}), bf16[8,64,512]{2,1,0:T(8,128)(2,1)}, u32[]{:S(2)}, u32[]{:S(2)}) async-start(bf16[8,64,512]{2,1,0:T(8,128)(2,1)} %get-tuple-element.745), calls=%async_computation.8 | async-start | bytes 1048576 | tf_op jit(solution)/shard_map/all_to_all | solution.py:390
  194.9 10.6 %conditional.10 = (bf16[8,64,512]{2,1,0:T(8,128)(2,1)}) conditional(s32[]{:T(128)} %clamp.21, (s32[5]{0:T(128)}, bf16[8,64,512]{2,1,0:T(8,128)(2,1)}, bf16[8,64,512]{2,1,0:T(8,128)(2,1)}, bf16[64,1024]{1,0:T(8,128)(2,1)}, bf16[64,1024]{1,0:T(8,128)(2,1)}, /*index=5*/bf16[64,1024]{1,0:T(8,128)(2,1)}) %tuple.108, (s32[5]{0:T(128)}, ...), branch_computations={%region_16.17_spmd, %region_17.18_spmd, %region_18.21_spmd} | conditional | flops 32774 | bytes 1507597 | solution.py:567
  205.5 5.2 %all-to-all-start.9 = ((bf16[8,64,512]{2,1,0:T(8,128)(2,1)}), bf16[8,64,512]{2,1,0:T(8,128)(2,1)}, u32[]{:S(2)}, u32[]{:S(2)}) async-start(bf16[8,64,512]{2,1,0:T(8,128)(2,1)} %get-tuple-element.1141.refs_8_), calls=%async_computation.9 | async-start | bytes 1048576 | tf_op jit(solution)/shard_map/all_to_all | solution.py:390
  217.8 6.1 %shard_map.79 = (bf16[8,64,512]{2,1,0:T(8,128)(2,1)}, bf16[64,1024]{1,0:T(8,128)(2,1)}, bf16[64,1024]{1,0:T(8,128)(2,1)}, bf16[64,1024]{1,0:T(8,128)(2,1)}, bf16[64,1024]{1,0:T(8,128)(2,1)}) custom-call(s32[5]{0:T(128)} %stack.23.ids, s32[2,8]{1,0:T(2,128)} %section_map.21, bf16[8,64,512]{2,1,0:T(8,128)(2,1)} %all-to-all-done.9.g_ref, ...), custom_call_target="tpu_custom_call" | custom-call | flops 536870912 | bytes 8388608 | tf_op jit(solution)/shard_map/pallas_call | solution.py:39
  236.8 19.6 %conditional.11 = (bf16[8,64,512]{2,1,0:T(8,128)(2,1)}) conditional(s32[]{:T(128)} %clamp.27, (s32[5]{0:T(128)}, bf16[8,64,512]{2,1,0:T(8,128)(2,1)}, bf16[8,64,512]{2,1,0:T(8,128)(2,1)}, bf16[64,1024]{1,0:T(8,128)(2,1)}, bf16[64,1024]{1,0:T(8,128)(2,1)}) %tuple.111, (s32[5]{0:T(128)}, bf16[8,64,512]{2,1,0:T(8,128)(2,1)}, ...), branch_computations={%region_21.22_spmd, %region_22.23_spmd, %region_23.26_spmd} | conditional | flops 32774 | bytes 1507597 | solution.py:567
  268.1 6.1 %shard_map.80 = (bf16[8,64,512]{2,1,0:T(8,128)(2,1)}, bf16[64,1024]{1,0:T(8,128)(2,1)}, bf16[64,1024]{1,0:T(8,128)(2,1)}, bf16[64,1024]{1,0:T(8,128)(2,1)}, bf16[64,1024]{1,0:T(8,128)(2,1)}) custom-call(s32[5]{0:T(128)} %stack.23.ids, s32[2,8]{1,0:T(2,128)} %section_map.21, bf16[8,64,512]{2,1,0:T(8,128)(2,1)} %all-to-all-done.11.g_ref, ...), custom_call_target="tpu_custom_call" | custom-call | flops 536870912 | bytes 8388608 | tf_op jit(solution)/shard_map/pallas_call | solution.py:39
  278.4 17.2 %collective-permute-start.42 = (bf16[8,64,768]{2,1,0:T(8,128)(2,1)}, bf16[8,64,768]{2,1,0:T(8,128)(2,1)}, u32[]{:S(2)}, u32[]{:S(2)}) collective-permute-start(bf16[8,64,768]{2,1,0:T(8,128)(2,1)} %collective-permute-done.41.refs_2_.refs_10_), channel_id=1, source_target_pairs={{0,8},{8,0},{16,24},{24,16},{32,40},{40,32},{48,56},{56,48},{1,9},... | collective-permute-start | bytes 2359304 | tf_op jit(solution)/shard_map/ppermute | solution.py:357
  305.2 10.3 %conditional.12 = (bf16[8,64,512]{2,1,0:T(8,128)(2,1)}) conditional(s32[]{:T(128)} %clamp.26, (s32[5]{0:T(128)}, bf16[8,64,512]{2,1,0:T(8,128)(2,1)}, bf16[8,64,512]{2,1,0:T(8,128)(2,1)}, bf16[64,1024]{1,0:T(8,128)(2,1)}, bf16[64,1024]{1,0:T(8,128)(2,1)}, /*index=5*/bf16[64,1024]{1,0:T(8,128)(2,1)}) %tuple.114, (s32[5]{0:T(128)}, ...), branch_computations={%region_26.27_spmd, %region_27.28_spmd, %region_28.31_spmd} | conditional | flops 32774 | bytes 1507597 | solution.py:567
  315.5 5.3 %all-to-all-start.13 = ((bf16[8,64,512]{2,1,0:T(8,128)(2,1)}), bf16[8,64,512]{2,1,0:T(8,128)(2,1)}, u32[]{:S(2)}, u32[]{:S(2)}) async-start(bf16[8,64,512]{2,1,0:T(8,128)(2,1)} %get-tuple-element.1143.refs_24_), calls=%async_computation.13 | async-start | bytes 1048576 | tf_op jit(solution)/shard_map/all_to_all | solution.py:390
  328.1 6.2 %shard_map.81 = (bf16[8,64,512]{2,1,0:T(8,128)(2,1)}, bf16[64,1536]{1,0:T(8,128)(2,1)}, bf16[64,1536]{1,0:T(8,128)(2,1)}, bf16[64,1536]{1,0:T(8,128)(2,1)}, bf16[64,1536]{1,0:T(8,128)(2,1)}) custom-call(s32[5]{0:T(128)} %stack.23.ids, s32[2,8]{1,0:T(2,128)} %section_map.21, bf16[8,64,512]{2,1,0:T(8,128)(2,1)} %all-to-all-done.13.g_ref, ...), custom_call_target="tpu_custom_call" | custom-call | flops 536870912 | bytes 8388608 | tf_op jit(solution)/shard_map/pallas_call | solution.py:39
  377.1 7.1 %collective-permute-start.59 = (bf16[2,64,768]{2,1,0:T(8,128)(2,1)}, bf16[2,64,768]{2,1,0:T(8,128)(2,1)}, u32[]{:S(2)}, u32[]{:S(2)}) collective-permute-start(bf16[2,64,768]{2,1,0:T(8,128)(2,1)} %get-tuple-element.779), channel_id=1, source_target_pairs={{0,8},{8,0},{16,24},{24,16},{32,40},{40,32},{48,56},{56,48},{1,9},... | collective-permute-start | bytes 589832 | tf_op jit(solution)/shard_map/ppermute | solution.py:357
  385.6 6.5 %shard_map.86 = (bf16[8,256,512]{2,1,0:T(8,128)(2,1)}, bf16[8,256,512]{2,1,0:T(8,128)(2,1)}) custom-call(s32[5]{0:T(128)} %stack.23.ids, bf16[8,64,640]{2,1,0:T(8,128)(2,1)} %get-tuple-element.749.refs_0_.refs_8_, bf16[8,64,640]{2,1,0:T(8,128)(2,1)} %collective-permute-done.40.refs_1_.refs_9_, bf16[8,64,768]{2,1,0:T(8,128)(2,1)} %collective-permute-done.41.refs_2_.refs_10_, ...), custom_call_target="tpu_custom_call" | custom-call | flops 805306368 | bytes 14400000 | tf_op jit(solution)/shard_map/pallas_call | solution.py:318
  (155 shorter events, 249.5 us)
Async XLA Ops:
  0.6 61.4 %collective-permute-start.26 = (bf16[2,4096,512]{2,1,0:T(8,128)(2,1)}, bf16[2,4096,512]{2,1,0:T(8,128)(2,1)}, u32[]{:S(2)}, u32[]{:S(2)}) collective-permute-start(bf16[2,4096,512]{2,1,0:T(8,128)(2,1)} %bitcast.34), channel_id=1, source_target_pairs={{0,8},{8,0},{16,24},{24,16},{32,40},{40,32},{48,56},{56,48},{1,9},... | collective-permute-start | bytes 25165832 | tf_op jit(solution)/shard_map/ppermute | solution.py:357
  2.1 59.9 %collective-permute-start.27 = (bf16[2,4096,512]{2,1,0:T(8,128)(2,1)}, bf16[2,4096,512]{2,1,0:T(8,128)(2,1)}, u32[]{:S(2)}, u32[]{:S(2)}) collective-permute-start(bf16[2,4096,512]{2,1,0:T(8,128)(2,1)} %bitcast.24), channel_id=1, source_target_pairs={{0,8},{8,0},{16,24},{24,16},{32,40},{40,32},{48,56},{56,48},{1,9},... | collective-permute-start | bytes 25165832 | tf_op jit(solution)/shard_map/ppermute | solution.py:357
  33.5 18.2 %all-to-all-start.1 = ((bf16[8,128,512]{2,1,0:T(8,128)(2,1)}), bf16[8,128,512]{2,1,0:T(8,128)(2,1)}, u32[]{:S(2)}, u32[]{:S(2)}) async-start(bf16[8,128,512]{2,1,0:T(8,128)(2,1)} %shard_map.70), calls=%async_computation.1 | async-start | bytes 2097152 | tf_op jit(solution)/shard_map/all_to_all | solution.py:390
  43.8 13.7 %collective-permute-start.16 = (bf16[2,64,1024]{2,1,0:T(8,128)(2,1)}, bf16[2,64,1024]{2,1,0:T(8,128)(2,1)}, u32[]{:S(2)}, u32[]{:S(2)}) collective-permute-start(bf16[2,64,1024]{2,1,0:T(8,128)(2,1)} %get-tuple-element.717.refs_3_), channel_id=1, source_target_pairs={{0,48},{8,56},{16,0},{24,8},{32,16},{40,24},{48,32},{56,40},{1,49}... | collective-permute-start | bytes 786440 | tf_op jit(solution)/shard_map/ppermute | solution.py:419
  46.4 13.0 %collective-permute-start.17 = (bf16[2,64,1024]{2,1,0:T(8,128)(2,1)}, bf16[2,64,1024]{2,1,0:T(8,128)(2,1)}, u32[]{:S(2)}, u32[]{:S(2)}) collective-permute-start(bf16[2,64,1024]{2,1,0:T(8,128)(2,1)} %get-tuple-element.718.refs_2_), channel_id=1, source_target_pairs={{0,32},{8,40},{16,48},{24,56},{32,0},{40,8},{48,16},{56,24},{1,33}... | collective-permute-start | bytes 786440 | tf_op jit(solution)/shard_map/ppermute | solution.py:419
  46.9 15.1 %collective-permute-start.18 = (bf16[2,64,1024]{2,1,0:T(8,128)(2,1)}, bf16[2,64,1024]{2,1,0:T(8,128)(2,1)}, u32[]{:S(2)}, u32[]{:S(2)}) collective-permute-start(bf16[2,64,1024]{2,1,0:T(8,128)(2,1)} %get-tuple-element.719.refs_1_), channel_id=1, source_target_pairs={{0,16},{8,24},{16,32},{24,40},{32,48},{40,56},{48,0},{56,8},{1,17}... | collective-permute-start | bytes 786440 | tf_op jit(solution)/shard_map/ppermute | solution.py:419
  68.3 14.4 %all-to-all-start.2 = ((bf16[8,64,512]{2,1,0:T(8,128)(2,1)}), bf16[8,64,512]{2,1,0:T(8,128)(2,1)}, u32[]{:S(2)}, u32[]{:S(2)}) async-start(bf16[8,64,512]{2,1,0:T(8,128)(2,1)} %get-tuple-element.733), calls=%async_computation.2 | async-start | bytes 1048576 | tf_op jit(solution)/shard_map/all_to_all | solution.py:390
  85.6 13.0 %all-to-all-start.3 = ((bf16[8,64,512]{2,1,0:T(8,128)(2,1)}), bf16[8,64,512]{2,1,0:T(8,128)(2,1)}, u32[]{:S(2)}, u32[]{:S(2)}) async-start(bf16[8,64,512]{2,1,0:T(8,128)(2,1)} %get-tuple-element.1138), calls=%async_computation.3 | async-start | bytes 1048576 | tf_op jit(solution)/shard_map/all_to_all | solution.py:390
  104.8 14.3 %all-to-all-start.4 = ((bf16[8,64,512]{2,1,0:T(8,128)(2,1)}), bf16[8,64,512]{2,1,0:T(8,128)(2,1)}, u32[]{:S(2)}, u32[]{:S(2)}) async-start(bf16[8,64,512]{2,1,0:T(8,128)(2,1)} %get-tuple-element.737), calls=%async_computation.4 | async-start | bytes 1048576 | tf_op jit(solution)/shard_map/all_to_all | solution.py:390
  146.8 12.4 %all-to-all-start.6 = ((bf16[8,64,512]{2,1,0:T(8,128)(2,1)}), bf16[8,64,512]{2,1,0:T(8,128)(2,1)}, u32[]{:S(2)}, u32[]{:S(2)}) async-start(bf16[8,64,512]{2,1,0:T(8,128)(2,1)} %get-tuple-element.740), calls=%async_computation.6 | async-start | bytes 1048576 | tf_op jit(solution)/shard_map/all_to_all | solution.py:390
  162.0 13.9 %all-to-all-start.7 = ((bf16[8,64,512]{2,1,0:T(8,128)(2,1)}), bf16[8,64,512]{2,1,0:T(8,128)(2,1)}, u32[]{:S(2)}, u32[]{:S(2)}) async-start(bf16[8,64,512]{2,1,0:T(8,128)(2,1)} %get-tuple-element.1140), calls=%async_computation.7 | async-start | bytes 1048576 | tf_op jit(solution)/shard_map/all_to_all | solution.py:390
  182.1 12.8 %all-to-all-start.8 = ((bf16[8,64,512]{2,1,0:T(8,128)(2,1)}), bf16[8,64,512]{2,1,0:T(8,128)(2,1)}, u32[]{:S(2)}, u32[]{:S(2)}) async-start(bf16[8,64,512]{2,1,0:T(8,128)(2,1)} %get-tuple-element.745), calls=%async_computation.8 | async-start | bytes 1048576 | tf_op jit(solution)/shard_map/all_to_all | solution.py:390
  224.0 12.9 %all-to-all-start.10 = ((bf16[8,64,512]{2,1,0:T(8,128)(2,1)}), bf16[8,64,512]{2,1,0:T(8,128)(2,1)}, u32[]{:S(2)}, u32[]{:S(2)}) async-start(bf16[8,64,512]{2,1,0:T(8,128)(2,1)} %get-tuple-element.752), calls=%async_computation.10 | async-start | bytes 1048576 | tf_op jit(solution)/shard_map/all_to_all | solution.py:390
  228.1 50.3 %collective-permute-start.41 = (bf16[8,64,768]{2,1,0:T(8,128)(2,1)}, bf16[8,64,768]{2,1,0:T(8,128)(2,1)}, u32[]{:S(2)}, u32[]{:S(2)}) collective-permute-start(bf16[8,64,768]{2,1,0:T(8,128)(2,1)} %get-tuple-element.751), channel_id=1, source_target_pairs={{0,64},{64,0},{1,65},{65,1},{2,66},{66,2},{3,67},{67,3},{4,68},{68... | collective-permute-start | bytes 2359304 | tf_op jit(solution)/shard_map/ppermute | solution.py:360
  274.3 30.9 %all-to-all-start.12 = ((bf16[8,64,512]{2,1,0:T(8,128)(2,1)}), bf16[8,64,512]{2,1,0:T(8,128)(2,1)}, u32[]{:S(2)}, u32[]{:S(2)}) async-start(bf16[8,64,512]{2,1,0:T(8,128)(2,1)} %get-tuple-element.756), calls=%async_computation.12 | async-start | bytes 1048576 | tf_op jit(solution)/shard_map/all_to_all | solution.py:390
  278.4 47.1 %collective-permute-start.42 = (bf16[8,64,768]{2,1,0:T(8,128)(2,1)}, bf16[8,64,768]{2,1,0:T(8,128)(2,1)}, u32[]{:S(2)}, u32[]{:S(2)}) collective-permute-start(bf16[8,64,768]{2,1,0:T(8,128)(2,1)} %collective-permute-done.41.refs_2_.refs_10_), channel_id=1, source_target_pairs={{0,8},{8,0},{16,24},{24,16},{32,40},{40,32},{48,56},{56,48},{1,9},... | collective-permute-start | bytes 2359304 | tf_op jit(solution)/shard_map/ppermute | solution.py:357
  295.7 29.8 %collective-permute-start.40 = (bf16[8,64,640]{2,1,0:T(8,128)(2,1)}, bf16[8,64,640]{2,1,0:T(8,128)(2,1)}, u32[]{:S(2)}, u32[]{:S(2)}) collective-permute-start(bf16[8,64,640]{2,1,0:T(8,128)(2,1)} %get-tuple-element.750), channel_id=1, source_target_pairs={{0,8},{8,0},{16,24},{24,16},{32,40},{40,32},{48,56},{56,48},{1,9},... | collective-permute-start | bytes 1966088 | tf_op jit(solution)/shard_map/ppermute | solution.py:357
  315.5 12.6 %all-to-all-start.13 = ((bf16[8,64,512]{2,1,0:T(8,128)(2,1)}), bf16[8,64,512]{2,1,0:T(8,128)(2,1)}, u32[]{:S(2)}, u32[]{:S(2)}) async-start(bf16[8,64,512]{2,1,0:T(8,128)(2,1)} %get-tuple-element.1143.refs_24_), calls=%async_computation.13 | async-start | bytes 1048576 | tf_op jit(solution)/shard_map/all_to_all | solution.py:390
  324.0 17.9 %collective-permute-start.54 = (bf16[6,64,768]{2,1,0:T(8,128)(2,1)}, bf16[6,64,768]{2,1,0:T(8,128)(2,1)}, u32[]{:S(2)}, u32[]{:S(2)}) collective-permute-start(bf16[6,64,768]{2,1,0:T(8,128)(2,1)} %get-tuple-element.772), channel_id=1, source_target_pairs={{0,64},{64,0},{1,65},{65,1},{2,66},{66,2},{3,67},{67,3},{4,68},{68... | collective-permute-start | bytes 1769480 | tf_op jit(solution)/shard_map/ppermute | solution.py:360
  334.3 12.4 %all-to-all-start.14 = ((bf16[8,64,512]{2,1,0:T(8,128)(2,1)}), bf16[8,64,512]{2,1,0:T(8,128)(2,1)}, u32[]{:S(2)}, u32[]{:S(2)}) async-start(bf16[8,64,512]{2,1,0:T(8,128)(2,1)} %get-tuple-element.760), calls=%async_computation.14 | async-start | bytes 1048576 | tf_op jit(solution)/shard_map/all_to_all | solution.py:390
  341.9 18.1 %collective-permute-start.55 = (bf16[6,64,768]{2,1,0:T(8,128)(2,1)}, bf16[6,64,768]{2,1,0:T(8,128)(2,1)}, u32[]{:S(2)}, u32[]{:S(2)}) collective-permute-start(bf16[6,64,768]{2,1,0:T(8,128)(2,1)} %collective-permute-done.54.refs_9_.refs_2_.refs_8_), channel_id=1, source_target_pairs={{0,8},{8,0},{16,24},{24,16},{32,40},{40,32},{48,56},{56,48},{1,9},... | collective-permute-start | bytes 1769480 | tf_op jit(solution)/shard_map/ppermute | solution.py:357
  345.0 13.0 %collective-permute-start.53 = (bf16[6,64,640]{2,1,0:T(8,128)(2,1)}, bf16[6,64,640]{2,1,0:T(8,128)(2,1)}, u32[]{:S(2)}, u32[]{:S(2)}) collective-permute-start(bf16[6,64,640]{2,1,0:T(8,128)(2,1)} %get-tuple-element.771), channel_id=1, source_target_pairs={{0,8},{8,0},{16,24},{24,16},{32,40},{40,32},{48,56},{56,48},{1,9},... | collective-permute-start | bytes 1474568 | tf_op jit(solution)/shard_map/ppermute | solution.py:357
  356.5 28.9 %collective-permute-start.43 = (bf16[4,8,64,128]{3,2,1,0:T(8,128)(2,1)}, bf16[4,8,64,128]{3,2,1,0:T(8,128)(2,1)}, u32[]{:S(2)}, u32[]{:S(2)}) collective-permute-start(bf16[4,8,64,128]{3,2,1,0:T(8,128)(2,1)} %shard_map.78.refs_4_), channel_id=1, source_target_pairs={{0,1},{1,0},{2,3},{3,2},{4,5},{5,4},{6,7},{7,6},{8,9},{9,8},{10,11... | collective-permute-start | bytes 1572872 | tf_op jit(solution)/shard_map/ppermute | solution.py:463
  369.4 16.0 %collective-permute-start.61 = (bf16[4,6,64,128]{3,2,1,0:T(8,128)(2,1)}, bf16[4,6,64,128]{3,2,1,0:T(8,128)(2,1)}, u32[]{:S(2)}, u32[]{:S(2)}) collective-permute-start(bf16[4,6,64,128]{3,2,1,0:T(8,128)(2,1)} %shard_map.85.refs_10_), channel_id=1, source_target_pairs={{0,1},{1,0},{2,3},{3,2},{4,5},{5,4},{6,7},{7,6},{8,9},{9,8},{10,11... | collective-permute-start | bytes 1179656 | tf_op jit(solution)/shard_map/ppermute | solution.py:463
  (44 other events, 267.9 us)

commit v2 on v1

--- a/solution.py
+++ b/solution.py
@@ -563,7 +563,7 @@
             mine = lax.fori_loop(0, most, hop, mine)
             return settle(mine, mine)
 
-        near = got_at[layer][1:] if layer in (5, 4, 2) else got_at[layer][1::2]
+        near = got_at[layer][1:]
         spread = lax.switch(jnp.minimum(most, 2), (stay, go_one, go_far), got, g, *near)
         g = over_tp(spread)
         if layer == 4:

time: 407 us -> 428 us (1.052)
  blocking collectives: 19.9 us -> 31.6 us
  waiting for transfers between devices: 96.3 us -> 102 us
  Pallas kernels: 118 us -> 123 us
    all_to_all x1 -> x2, blocking collectives: 19.9 us -> 31.6 us  [over_tp(): return lax.all_to_all(parts, 'tp', 0, 0, tiled=True)]
    ppermute x4 -> x6, waiting for transfers between devices: 16.5 us -> 25.2 us  [go_one(): return settle(mine, lax.ppermute(mine, 'section', down))]
    ppermute x14, starting transfers between devices: 36.8 us -> 42.5 us  [to_sibling(): return lax.ppermute(array, 'section', swap)]
    pallas_call x29 -> x31, Pallas kernels: 109 us -> 114 us  [run(): pl.pallas_call(kernel, out_shape=outs, in_specs=specs, out_specs=out_spec...]
    all_to_all x15 -> x14, starting transfers between devices: 70.3 us -> 66.3 us  [over_tp(): return lax.all_to_all(parts, 'tp', 0, 0, tiled=True)]
    all_to_all x15 -> x14, waiting for transfers between devices: 17.7 us -> 18.9 us  [over_tp(): return lax.all_to_all(parts, 'tp', 0, 0, tiled=True)]
  transfers between devices with their start and end apart: 68 -> 69, of which waited for: 46 -> 45; matrix products, arithmetic and copies ran while one was open for 1% -> 1% of each run, Pallas kernels for 17% -> 17%
where the time goes in v2:
time: 428 us; the launch traced here: 424 us
  starting transfers between devices  150 us (35%)
  Pallas kernels  123 us (29%)
  waiting for transfers between devices  102 us (24%)
  blocking collectives  31.6 us (7%)
  loops' own time  9.34 us (2%)
  between operations  5.7 us (1%)
    pallas_call x31, Pallas kernels, run(): pl.pallas_call(kernel, out_shape=outs, in_specs=specs, out_specs=out_spec...  114 us
    all_to_all x14, starting transfers between devices, over_tp(): return lax.all_to_all(parts, 'tp', 0, 0, tiled=True)  66.3 us
    ppermute x30, waiting for transfers between devices, along_chips(): got.append(lax.ppermute(cuts[back], 'section', route))  50.6 us
    ppermute x14, starting transfers between devices, to_sibling(): return lax.ppermute(array, 'section', swap)  42.5 us
    all_to_all x2, blocking collectives, over_tp(): return lax.all_to_all(parts, 'tp', 0, 0, tiled=True)  31.6 us
    ppermute x30, starting transfers between devices, along_chips(): got.append(lax.ppermute(cuts[back], 'section', route))  25.7 us
    ppermute x6, waiting for transfers between devices, go_one(): return settle(mine, lax.ppermute(mine, 'section', down))  25.2 us
    all_to_all x14, waiting for transfers between devices, over_tp(): return lax.all_to_all(parts, 'tp', 0, 0, tiled=True)  18.9 us
  transfers between devices with their start and end apart: 69, of which 45 were waited for; matrix products, arithmetic and copies ran while one was open for 1% of the time, Pallas kernels for 17%

profile of v2, /device:TPU:1, one launch (start us, length us, event | category | flops | bytes accessed | tf_op | source)
XLA Modules:
  0.0 424.1 jit_solution(14193704892711663405)
XLA Ops:
  2.9 7.6 %shard_map.68 = (bf16[8,128,512]{2,1,0:T(8,128)(2,1)}, bf16[64,512]{1,0:T(8,128)(2,1)}, bf16[64,512]{1,0:T(8,128)(2,1)}, f32[64,512]{1,0:T(8,128)}, f32[64,512]{...) custom-call(s32[5]{0:T(128)} %stack.23.ids, bf16[128,4096]{1,0:T(8,128)(2,1)} %bitcast.48, ...), custom_call_target="tpu_custom_call" | custom-call | flops 1073741824 | bytes 8388608 | tf_op jit(solution)/shard_map/pallas_call | solution.py:39
  10.4 19.9 %all_to_all.80.got_ref = bf16[8,128,512]{2,1,0:T(8,128)(2,1)} all-to-all(bf16[8,128,512]{2,1,0:T(8,128)(2,1)} %get-tuple-element.756), channel_id=1, replica_groups=mesh['rep'=2,'section'=8,'tp'=8] {'tp'}, dimensions={0} | all-to-all | bytes 2097152 | tf_op jit(solution)/shard_map/all_to_all | solution.py:390
  62.0 6.3 %shard_map.73 = (bf16[8,64,512]{2,1,0:T(8,128)(2,1)}, bf16[64,1024]{1,0:T(8,128)(2,1)}, bf16[64,1024]{1,0:T(8,128)(2,1)}, bf16[64,1024]{1,0:T(8,128)(2,1)}, bf16[64,1024]{1,0:T(8,128)(2,1)}) custom-call(s32[5]{0:T(128)} %stack.23.ids, s32[2,8]{1,0:T(2,128)} %section_map.21, bf16[2,64,4096]{2,1,0:T(8,128)(2,1)} %bitcast.44, ...), custom_call_target="tpu_custom_call" | custom-call | flops 536870912 | bytes 8388608 | tf_op jit(solution)/shard_map/pallas_call | solution.py:39
  68.3 5.3 %all-to-all-start.2 = ((bf16[8,64,512]{2,1,0:T(8,128)(2,1)}), bf16[8,64,512]{2,1,0:T(8,128)(2,1)}, u32[]{:S(2)}, u32[]{:S(2)}) async-start(bf16[8,64,512]{2,1,0:T(8,128)(2,1)} %get-tuple-element.769), calls=%async_computation.2 | async-start | bytes 1048576 | tf_op jit(solution)/shard_map/all_to_all | solution.py:390
  88.0 5.1 %all-to-all-start.3 = ((bf16[8,64,512]{2,1,0:T(8,128)(2,1)}), bf16[8,64,512]{2,1,0:T(8,128)(2,1)}, u32[]{:S(2)}, u32[]{:S(2)}) async-start(bf16[8,64,512]{2,1,0:T(8,128)(2,1)} %get-tuple-element.1174), calls=%async_computation.3 | async-start | bytes 1048576 | tf_op jit(solution)/shard_map/all_to_all | solution.py:390
  101.9 6.2 %shard_map.74 = (bf16[8,64,512]{2,1,0:T(8,128)(2,1)}, bf16[64,1024]{1,0:T(8,128)(2,1)}, bf16[64,1024]{1,0:T(8,128)(2,1)}, bf16[64,1024]{1,0:T(8,128)(2,1)}, bf16[64,1024]{1,0:T(8,128)(2,1)}) custom-call(s32[5]{0:T(128)} %stack.23.ids, s32[2,8]{1,0:T(2,128)} %section_map.21, bf16[8,64,512]{2,1,0:T(8,128)(2,1)} %all-to-all-done.3.g_ref, ...), custom_call_target="tpu_custom_call" | custom-call | flops 536870912 | bytes 8388608 | tf_op jit(solution)/shard_map/pallas_call | solution.py:39
  120.3 10.3 %conditional.8 = (bf16[8,64,512]{2,1,0:T(8,128)(2,1)}) conditional(s32[]{:T(128)} %clamp.23, (s32[5]{0:T(128)}, bf16[8,64,512]{2,1,0:T(8,128)(2,1)}, bf16[8,64,512]{2,1,0:T(8,128)(2,1)}, bf16[64,1024]{1,0:T(8,128)(2,1)}, bf16[64,1024]{1,0:T(8,128)(2,1)}, /*index=5*/bf16[64,1024]{1,0:T(8,128)(2,1)}) %tuple.102, (s32[5]{0:T(128)}, ...), branch_computations={%region_6.7_spmd, %region_7.8_spmd, %region_8.11_spmd} | conditional | flops 32774 | bytes 1507597 | solution.py:567
  142.3 6.2 %shard_map.75 = (bf16[8,64,512]{2,1,0:T(8,128)(2,1)}, bf16[64,1024]{1,0:T(8,128)(2,1)}, bf16[64,1024]{1,0:T(8,128)(2,1)}, bf16[64,1024]{1,0:T(8,128)(2,1)}, bf16[64,1024]{1,0:T(8,128)(2,1)}) custom-call(s32[5]{0:T(128)} %stack.23.ids, s32[2,8]{1,0:T(2,128)} %section_map.21, bf16[8,64,512]{2,1,0:T(8,128)(2,1)} %all-to-all-done.5.g_ref, ...), custom_call_target="tpu_custom_call" | custom-call | flops 536870912 | bytes 8388608 | tf_op jit(solution)/shard_map/pallas_call | solution.py:39
  161.0 10.3 %conditional.9 = (bf16[8,64,512]{2,1,0:T(8,128)(2,1)}) conditional(s32[]{:T(128)} %clamp.22, (s32[5]{0:T(128)}, bf16[8,64,512]{2,1,0:T(8,128)(2,1)}, bf16[8,64,512]{2,1,0:T(8,128)(2,1)}, bf16[64,1024]{1,0:T(8,128)(2,1)}, bf16[64,1024]{1,0:T(8,128)(2,1)}, /*index=5*/bf16[64,1024]{1,0:T(8,128)(2,1)}) %tuple.105, (s32[5]{0:T(128)}, ...), branch_computations={%region_11.12_spmd, %region_12.13_spmd, %region_13.16_spmd} | conditional | flops 32774 | bytes 1507597 | solution.py:567
  171.3 5.3 %all-to-all-start.7 = ((bf16[8,64,512]{2,1,0:T(8,128)(2,1)}), bf16[8,64,512]{2,1,0:T(8,128)(2,1)}, u32[]{:S(2)}, u32[]{:S(2)}) async-start(bf16[8,64,512]{2,1,0:T(8,128)(2,1)} %get-tuple-element.1176), calls=%async_computation.7 | async-start | bytes 1048576 | tf_op jit(solution)/shard_map/all_to_all | solution.py:390
  178.1 5.5 %collective-permute-done.22.refs_8_.refs_6_ = bf16[2,64,1024]{2,1,0:T(8,128)(2,1)} collective-permute-done((bf16[2,64,1024]{2,1,0:T(8,128)(2,1)}, bf16[2,64,1024]{2,1,0:T(8,128)(2,1)}, u32[]{:S(2)}, u32[]{:S(2)}) %collective-permute-start.22) | collective-permute-done | bytes 262176 | tf_op jit(solution)/shard_map/ppermute | solution.py:419
  183.7 6.2 %shard_map.76 = (bf16[8,64,512]{2,1,0:T(8,128)(2,1)}, bf16[64,1024]{1,0:T(8,128)(2,1)}, bf16[64,1024]{1,0:T(8,128)(2,1)}, bf16[64,1024]{1,0:T(8,128)(2,1)}, bf16[64,1024]{1,0:T(8,128)(2,1)}) custom-call(s32[5]{0:T(128)} %stack.23.ids, s32[2,8]{1,0:T(2,128)} %section_map.21, bf16[8,64,512]{2,1,0:T(8,128)(2,1)} %all-to-all-done.7.g_ref, ...), custom_call_target="tpu_custom_call" | custom-call | flops 536870912 | bytes 8388608 | tf_op jit(solution)/shard_map/pallas_call | solution.py:39
  202.2 11.2 %conditional.10 = (bf16[8,64,512]{2,1,0:T(8,128)(2,1)}) conditional(s32[]{:T(128)} %clamp.21, (s32[5]{0:T(128)}, bf16[8,64,512]{2,1,0:T(8,128)(2,1)}, bf16[8,64,512]{2,1,0:T(8,128)(2,1)}, bf16[64,1024]{1,0:T(8,128)(2,1)}, bf16[64,1024]{1,0:T(8,128)(2,1)}, /*index=5*/bf16[64,1024]{1,0:T(8,128)(2,1)}) %tuple.108, (s32[5]{0:T(128)}, ...), branch_computations={%region_16.17_spmd, %region_17.18_spmd, %region_18.21_spmd} | conditional | flops 32774 | bytes 1507597 | solution.py:567
  225.4 6.2 %shard_map.79 = (bf16[8,64,512]{2,1,0:T(8,128)(2,1)}, bf16[64,1024]{1,0:T(8,128)(2,1)}, bf16[64,1024]{1,0:T(8,128)(2,1)}, bf16[64,1024]{1,0:T(8,128)(2,1)}, bf16[64,1024]{1,0:T(8,128)(2,1)}) custom-call(s32[5]{0:T(128)} %stack.23.ids, s32[2,8]{1,0:T(2,128)} %section_map.21, bf16[8,64,512]{2,1,0:T(8,128)(2,1)} %all-to-all-done.9.g_ref, ...), custom_call_target="tpu_custom_call" | custom-call | flops 536870912 | bytes 8388608 | tf_op jit(solution)/shard_map/pallas_call | solution.py:39
  246.7 19.8 %conditional.11 = (bf16[8,64,512]{2,1,0:T(8,128)(2,1)}) conditional(s32[]{:T(128)} %clamp.27, (s32[5]{0:T(128)}, bf16[8,64,512]{2,1,0:T(8,128)(2,1)}, bf16[8,64,512]{2,1,0:T(8,128)(2,1)}, bf16[64,1024]{1,0:T(8,128)(2,1)}, bf16[64,1024]{1,0:T(8,128)(2,1)}, /*index=5*/bf16[64,1024]{1,0:T(8,128)(2,1)}) %tuple.111, (s32[5]{0:T(128)}, ...), branch_computations={%region_21.22_spmd, %region_22.23_spmd, %region_23.26_spmd} | conditional | flops 32774 | bytes 1507597 | solution.py:567
  266.5 11.7 %all_to_all.81.g_ref = bf16[8,64,512]{2,1,0:T(8,128)(2,1)} all-to-all(bf16[8,64,512]{2,1,0:T(8,128)(2,1)} %get-tuple-element.1178), channel_id=1, replica_groups=mesh['rep'=2,'section'=8,'tp'=8] {'tp'}, dimensions={0} | all-to-all | bytes 1048576 | tf_op jit(solution)/shard_map/all_to_all | solution.py:390
  278.2 6.2 %shard_map.80 = (bf16[8,64,512]{2,1,0:T(8,128)(2,1)}, bf16[64,1024]{1,0:T(8,128)(2,1)}, bf16[64,1024]{1,0:T(8,128)(2,1)}, bf16[64,1024]{1,0:T(8,128)(2,1)}, bf16[64,1024]{1,0:T(8,128)(2,1)}) custom-call(s32[5]{0:T(128)} %stack.23.ids, s32[2,8]{1,0:T(2,128)} %section_map.21, bf16[8,64,512]{2,1,0:T(8,128)(2,1)} %all_to_all.81.g_ref, ...), custom_call_target="tpu_custom_call" | custom-call | flops 536870912 | bytes 8388608 | tf_op jit(solution)/shard_map/pallas_call | solution.py:39
  288.5 21.1 %collective-permute-start.42 = (bf16[8,64,768]{2,1,0:T(8,128)(2,1)}, bf16[8,64,768]{2,1,0:T(8,128)(2,1)}, u32[]{:S(2)}, u32[]{:S(2)}) collective-permute-start(bf16[8,64,768]{2,1,0:T(8,128)(2,1)} %collective-permute-done.41.refs_2_.refs_10_), channel_id=1, source_target_pairs={{0,8},{8,0},{16,24},{24,16},{32,40},{40,32},{48,56},{56,48},{1,9},... | collective-permute-start | bytes 2359304 | tf_op jit(solution)/shard_map/ppermute | solution.py:357
  319.3 10.3 %conditional.12 = (bf16[8,64,512]{2,1,0:T(8,128)(2,1)}) conditional(s32[]{:T(128)} %clamp.26, (s32[5]{0:T(128)}, bf16[8,64,512]{2,1,0:T(8,128)(2,1)}, bf16[8,64,512]{2,1,0:T(8,128)(2,1)}, bf16[64,1024]{1,0:T(8,128)(2,1)}, bf16[64,1024]{1,0:T(8,128)(2,1)}, /*index=5*/bf16[64,1024]{1,0:T(8,128)(2,1)}) %tuple.114, (s32[5]{0:T(128)}, ...), branch_computations={%region_26.27_spmd, %region_27.28_spmd, %region_28.31_spmd} | conditional | flops 32774 | bytes 1507597 | solution.py:567
  329.6 5.2 %all-to-all-start.13 = ((bf16[8,64,512]{2,1,0:T(8,128)(2,1)}), bf16[8,64,512]{2,1,0:T(8,128)(2,1)}, u32[]{:S(2)}, u32[]{:S(2)}) async-start(bf16[8,64,512]{2,1,0:T(8,128)(2,1)} %get-tuple-element.1179.refs_24_), calls=%async_computation.13 | async-start | bytes 1048576 | tf_op jit(solution)/shard_map/all_to_all | solution.py:390
  342.1 6.2 %shard_map.81 = (bf16[8,64,512]{2,1,0:T(8,128)(2,1)}, bf16[64,1536]{1,0:T(8,128)(2,1)}, bf16[64,1536]{1,0:T(8,128)(2,1)}, bf16[64,1536]{1,0:T(8,128)(2,1)}, bf16[64,1536]{1,0:T(8,128)(2,1)}) custom-call(s32[5]{0:T(128)} %stack.23.ids, s32[2,8]{1,0:T(2,128)} %section_map.21, bf16[8,64,512]{2,1,0:T(8,128)(2,1)} %all-to-all-done.13.g_ref, ...), custom_call_target="tpu_custom_call" | custom-call | flops 536870912 | bytes 8388608 | tf_op jit(solution)/shard_map/pallas_call | solution.py:39
  361.0 10.3 %conditional.13 = (bf16[8,64,512]{2,1,0:T(8,128)(2,1)}) conditional(s32[]{:T(128)} %clamp.25, (s32[5]{0:T(128)}, bf16[8,64,512]{2,1,0:T(8,128)(2,1)}, bf16[8,64,512]{2,1,0:T(8,128)(2,1)}, bf16[64,1536]{1,0:T(8,128)(2,1)}, bf16[64,1536]{1,0:T(8,128)(2,1)}, /*index=5*/bf16[64,1536]{1,0:T(8,128)(2,1)}) %tuple.117, (s32[5]{0:T(128)}, ...), branch_computations={%region_31.32_spmd, %region_32.33_spmd, %region_33.36_spmd} | conditional | flops 32774 | bytes 1507589 | solution.py:567
  400.2 8.9 %collective-permute-start.59 = (bf16[2,64,768]{2,1,0:T(8,128)(2,1)}, bf16[2,64,768]{2,1,0:T(8,128)(2,1)}, u32[]{:S(2)}, u32[]{:S(2)}) collective-permute-start(bf16[2,64,768]{2,1,0:T(8,128)(2,1)} %get-tuple-element.815), channel_id=1, source_target_pairs={{0,8},{8,0},{16,24},{24,16},{32,40},{40,32},{48,56},{56,48},{1,9},... | collective-permute-start | bytes 589832 | tf_op jit(solution)/shard_map/ppermute | solution.py:357
  410.5 6.5 %shard_map.86 = (bf16[8,256,512]{2,1,0:T(8,128)(2,1)}, bf16[8,256,512]{2,1,0:T(8,128)(2,1)}) custom-call(s32[5]{0:T(128)} %stack.23.ids, bf16[8,64,640]{2,1,0:T(8,128)(2,1)} %get-tuple-element.785.refs_0_.refs_8_, bf16[8,64,640]{2,1,0:T(8,128)(2,1)} %collective-permute-done.40.refs_1_.refs_9_, bf16[8,64,768]{2,1,0:T(8,128)(2,1)} %collective-permute-done.41.refs_2_.refs_10_, ...), custom_call_target="tpu_custom_call" | custom-call | flops 805306368 | bytes 14400000 | tf_op jit(solution)/shard_map/pallas_call | solution.py:318
  (160 shorter events, 266.5 us)
Async XLA Ops:
  0.6 61.4 %collective-permute-start.26 = (bf16[2,4096,512]{2,1,0:T(8,128)(2,1)}, bf16[2,4096,512]{2,1,0:T(8,128)(2,1)}, u32[]{:S(2)}, u32[]{:S(2)}) collective-permute-start(bf16[2,4096,512]{2,1,0:T(8,128)(2,1)} %bitcast.34), channel_id=1, source_target_pairs={{0,8},{8,0},{16,24},{24,16},{32,40},{40,32},{48,56},{56,48},{1,9},... | collective-permute-start | bytes 25165832 | tf_op jit(solution)/shard_map/ppermute | solution.py:357
  2.1 59.9 %collective-permute-start.27 = (bf16[2,4096,512]{2,1,0:T(8,128)(2,1)}, bf16[2,4096,512]{2,1,0:T(8,128)(2,1)}, u32[]{:S(2)}, u32[]{:S(2)}) collective-permute-start(bf16[2,4096,512]{2,1,0:T(8,128)(2,1)} %bitcast.24), channel_id=1, source_target_pairs={{0,8},{8,0},{16,24},{24,16},{32,40},{40,32},{48,56},{56,48},{1,9},... | collective-permute-start | bytes 25165832 | tf_op jit(solution)/shard_map/ppermute | solution.py:357
  33.5 18.3 %all-to-all-start.1 = ((bf16[8,128,512]{2,1,0:T(8,128)(2,1)}), bf16[8,128,512]{2,1,0:T(8,128)(2,1)}, u32[]{:S(2)}, u32[]{:S(2)}) async-start(bf16[8,128,512]{2,1,0:T(8,128)(2,1)} %shard_map.70), calls=%async_computation.1 | async-start | bytes 2097152 | tf_op jit(solution)/shard_map/all_to_all | solution.py:390
  43.8 13.6 %collective-permute-start.16 = (bf16[2,64,1024]{2,1,0:T(8,128)(2,1)}, bf16[2,64,1024]{2,1,0:T(8,128)(2,1)}, u32[]{:S(2)}, u32[]{:S(2)}) collective-permute-start(bf16[2,64,1024]{2,1,0:T(8,128)(2,1)} %get-tuple-element.753.refs_3_), channel_id=1, source_target_pairs={{0,48},{8,56},{16,0},{24,8},{32,16},{40,24},{48,32},{56,40},{1,49}... | collective-permute-start | bytes 786440 | tf_op jit(solution)/shard_map/ppermute | solution.py:419
  46.4 13.0 %collective-permute-start.17 = (bf16[2,64,1024]{2,1,0:T(8,128)(2,1)}, bf16[2,64,1024]{2,1,0:T(8,128)(2,1)}, u32[]{:S(2)}, u32[]{:S(2)}) collective-permute-start(bf16[2,64,1024]{2,1,0:T(8,128)(2,1)} %get-tuple-element.754.refs_2_), channel_id=1, source_target_pairs={{0,32},{8,40},{16,48},{24,56},{32,0},{40,8},{48,16},{56,24},{1,33}... | collective-permute-start | bytes 786440 | tf_op jit(solution)/shard_map/ppermute | solution.py:419
  46.9 15.1 %collective-permute-start.18 = (bf16[2,64,1024]{2,1,0:T(8,128)(2,1)}, bf16[2,64,1024]{2,1,0:T(8,128)(2,1)}, u32[]{:S(2)}, u32[]{:S(2)}) collective-permute-start(bf16[2,64,1024]{2,1,0:T(8,128)(2,1)} %get-tuple-element.755.refs_1_), channel_id=1, source_target_pairs={{0,16},{8,24},{16,32},{24,40},{32,48},{40,56},{48,0},{56,8},{1,17}... | collective-permute-start | bytes 786440 | tf_op jit(solution)/shard_map/ppermute | solution.py:419
  68.3 16.9 %all-to-all-start.2 = ((bf16[8,64,512]{2,1,0:T(8,128)(2,1)}), bf16[8,64,512]{2,1,0:T(8,128)(2,1)}, u32[]{:S(2)}, u32[]{:S(2)}) async-start(bf16[8,64,512]{2,1,0:T(8,128)(2,1)} %get-tuple-element.769), calls=%async_computation.2 | async-start | bytes 1048576 | tf_op jit(solution)/shard_map/all_to_all | solution.py:390
  88.0 13.9 %all-to-all-start.3 = ((bf16[8,64,512]{2,1,0:T(8,128)(2,1)}), bf16[8,64,512]{2,1,0:T(8,128)(2,1)}, u32[]{:S(2)}, u32[]{:S(2)}) async-start(bf16[8,64,512]{2,1,0:T(8,128)(2,1)} %get-tuple-element.1174), calls=%async_computation.3 | async-start | bytes 1048576 | tf_op jit(solution)/shard_map/all_to_all | solution.py:390
  148.5 12.5 %all-to-all-start.6 = ((bf16[8,64,512]{2,1,0:T(8,128)(2,1)}), bf16[8,64,512]{2,1,0:T(8,128)(2,1)}, u32[]{:S(2)}, u32[]{:S(2)}) async-start(bf16[8,64,512]{2,1,0:T(8,128)(2,1)} %get-tuple-element.777), calls=%async_computation.6 | async-start | bytes 1048576 | tf_op jit(solution)/shard_map/all_to_all | solution.py:390
  171.3 12.5 %all-to-all-start.7 = ((bf16[8,64,512]{2,1,0:T(8,128)(2,1)}), bf16[8,64,512]{2,1,0:T(8,128)(2,1)}, u32[]{:S(2)}, u32[]{:S(2)}) async-start(bf16[8,64,512]{2,1,0:T(8,128)(2,1)} %get-tuple-element.1176), calls=%async_computation.7 | async-start | bytes 1048576 | tf_op jit(solution)/shard_map/all_to_all | solution.py:390
  189.9 12.3 %all-to-all-start.8 = ((bf16[8,64,512]{2,1,0:T(8,128)(2,1)}), bf16[8,64,512]{2,1,0:T(8,128)(2,1)}, u32[]{:S(2)}, u32[]{:S(2)}) async-start(bf16[8,64,512]{2,1,0:T(8,128)(2,1)} %get-tuple-element.781), calls=%async_computation.8 | async-start | bytes 1048576 | tf_op jit(solution)/shard_map/all_to_all | solution.py:390
  231.6 15.1 %all-to-all-start.10 = ((bf16[8,64,512]{2,1,0:T(8,128)(2,1)}), bf16[8,64,512]{2,1,0:T(8,128)(2,1)}, u32[]{:S(2)}, u32[]{:S(2)}) async-start(bf16[8,64,512]{2,1,0:T(8,128)(2,1)} %get-tuple-element.788), calls=%async_computation.10 | async-start | bytes 1048576 | tf_op jit(solution)/shard_map/all_to_all | solution.py:390
  235.7 52.8 %collective-permute-start.41 = (bf16[8,64,768]{2,1,0:T(8,128)(2,1)}, bf16[8,64,768]{2,1,0:T(8,128)(2,1)}, u32[]{:S(2)}, u32[]{:S(2)}) collective-permute-start(bf16[8,64,768]{2,1,0:T(8,128)(2,1)} %get-tuple-element.787), channel_id=1, source_target_pairs={{0,64},{64,0},{1,65},{65,1},{2,66},{66,2},{3,67},{67,3},{4,68},{68... | collective-permute-start | bytes 2359304 | tf_op jit(solution)/shard_map/ppermute | solution.py:360
  284.3 34.9 %all-to-all-start.12 = ((bf16[8,64,512]{2,1,0:T(8,128)(2,1)}), bf16[8,64,512]{2,1,0:T(8,128)(2,1)}, u32[]{:S(2)}, u32[]{:S(2)}) async-start(bf16[8,64,512]{2,1,0:T(8,128)(2,1)} %get-tuple-element.792), calls=%async_computation.12 | async-start | bytes 1048576 | tf_op jit(solution)/shard_map/all_to_all | solution.py:390
  288.5 50.5 %collective-permute-start.42 = (bf16[8,64,768]{2,1,0:T(8,128)(2,1)}, bf16[8,64,768]{2,1,0:T(8,128)(2,1)}, u32[]{:S(2)}, u32[]{:S(2)}) collective-permute-start(bf16[8,64,768]{2,1,0:T(8,128)(2,1)} %collective-permute-done.41.refs_2_.refs_10_), channel_id=1, source_target_pairs={{0,8},{8,0},{16,24},{24,16},{32,40},{40,32},{48,56},{56,48},{1,9},... | collective-permute-start | bytes 2359304 | tf_op jit(solution)/shard_map/ppermute | solution.py:357
  309.6 29.4 %collective-permute-start.40 = (bf16[8,64,640]{2,1,0:T(8,128)(2,1)}, bf16[8,64,640]{2,1,0:T(8,128)(2,1)}, u32[]{:S(2)}, u32[]{:S(2)}) collective-permute-start(bf16[8,64,640]{2,1,0:T(8,128)(2,1)} %get-tuple-element.786), channel_id=1, source_target_pairs={{0,8},{8,0},{16,24},{24,16},{32,40},{40,32},{48,56},{56,48},{1,9},... | collective-permute-start | bytes 1966088 | tf_op jit(solution)/shard_map/ppermute | solution.py:357
  329.6 12.5 %all-to-all-start.13 = ((bf16[8,64,512]{2,1,0:T(8,128)(2,1)}), bf16[8,64,512]{2,1,0:T(8,128)(2,1)}, u32[]{:S(2)}, u32[]{:S(2)}) async-start(bf16[8,64,512]{2,1,0:T(8,128)(2,1)} %get-tuple-element.1179.refs_24_), calls=%async_computation.13 | async-start | bytes 1048576 | tf_op jit(solution)/shard_map/all_to_all | solution.py:390
  338.0 17.5 %collective-permute-start.54 = (bf16[6,64,768]{2,1,0:T(8,128)(2,1)}, bf16[6,64,768]{2,1,0:T(8,128)(2,1)}, u32[]{:S(2)}, u32[]{:S(2)}) collective-permute-start(bf16[6,64,768]{2,1,0:T(8,128)(2,1)} %get-tuple-element.808), channel_id=1, source_target_pairs={{0,64},{64,0},{1,65},{65,1},{2,66},{66,2},{3,67},{67,3},{4,68},{68... | collective-permute-start | bytes 1769480 | tf_op jit(solution)/shard_map/ppermute | solution.py:360
  348.2 12.8 %all-to-all-start.14 = ((bf16[8,64,512]{2,1,0:T(8,128)(2,1)}), bf16[8,64,512]{2,1,0:T(8,128)(2,1)}, u32[]{:S(2)}, u32[]{:S(2)}) async-start(bf16[8,64,512]{2,1,0:T(8,128)(2,1)} %get-tuple-element.796), calls=%async_computation.14 | async-start | bytes 1048576 | tf_op jit(solution)/shard_map/all_to_all | solution.py:390
  355.5 24.4 %collective-permute-start.55 = (bf16[6,64,768]{2,1,0:T(8,128)(2,1)}, bf16[6,64,768]{2,1,0:T(8,128)(2,1)}, u32[]{:S(2)}, u32[]{:S(2)}) collective-permute-start(bf16[6,64,768]{2,1,0:T(8,128)(2,1)} %collective-permute-done.54.refs_9_.refs_2_.refs_8_), channel_id=1, source_target_pairs={{0,8},{8,0},{16,24},{24,16},{32,40},{40,32},{48,56},{56,48},{1,9},... | collective-permute-start | bytes 1769480 | tf_op jit(solution)/shard_map/ppermute | solution.py:357
  359.6 20.2 %collective-permute-start.53 = (bf16[6,64,640]{2,1,0:T(8,128)(2,1)}, bf16[6,64,640]{2,1,0:T(8,128)(2,1)}, u32[]{:S(2)}, u32[]{:S(2)}) collective-permute-start(bf16[6,64,640]{2,1,0:T(8,128)(2,1)} %get-tuple-element.807), channel_id=1, source_target_pairs={{0,8},{8,0},{16,24},{24,16},{32,40},{40,32},{48,56},{56,48},{1,9},... | collective-permute-start | bytes 1474568 | tf_op jit(solution)/shard_map/ppermute | solution.py:357
  371.3 12.3 %all-to-all-start.15 = ((bf16[8,64,512]{2,1,0:T(8,128)(2,1)}), bf16[8,64,512]{2,1,0:T(8,128)(2,1)}, u32[]{:S(2)}, u32[]{:S(2)}) async-start(bf16[8,64,512]{2,1,0:T(8,128)(2,1)} %get-tuple-element.1180), calls=%async_computation.15 | async-start | bytes 1048576 | tf_op jit(solution)/shard_map/all_to_all | solution.py:390
  378.3 31.8 %collective-permute-start.43 = (bf16[4,8,64,128]{3,2,1,0:T(8,128)(2,1)}, bf16[4,8,64,128]{3,2,1,0:T(8,128)(2,1)}, u32[]{:S(2)}, u32[]{:S(2)}) collective-permute-start(bf16[4,8,64,128]{3,2,1,0:T(8,128)(2,1)} %shard_map.78.refs_4_), channel_id=1, source_target_pairs={{0,1},{1,0},{2,3},{3,2},{4,5},{5,4},{6,7},{7,6},{8,9},{9,8},{10,11... | collective-permute-start | bytes 1572872 | tf_op jit(solution)/shard_map/ppermute | solution.py:463
  393.3 16.7 %collective-permute-start.61 = (bf16[4,6,64,128]{3,2,1,0:T(8,128)(2,1)}, bf16[4,6,64,128]{3,2,1,0:T(8,128)(2,1)}, u32[]{:S(2)}, u32[]{:S(2)}) collective-permute-start(bf16[4,6,64,128]{3,2,1,0:T(8,128)(2,1)} %shard_map.85.refs_10_), channel_id=1, source_target_pairs={{0,1},{1,0},{2,3},{3,2},{4,5},{5,4},{6,7},{7,6},{8,9},{9,8},{10,11... | collective-permute-start | bytes 1179656 | tf_op jit(solution)/shard_map/ppermute | solution.py:463
  (45 other events, 276.1 us)
